TPU v7x, 256 devices: a whole 4x4x8 slice. The times are simulated.
256 devices in a mesh: lon: 16 (over z, y_lo), lat: 16 (over y_hi, x, core).
Axes of the slice: x: 4, y: 4 (y_hi: 2, y_lo: 2; y = y_hi * 2 + y_lo), z: 8, core: 2. Of those that a mesh axis runs over, the one named last changes fastest.
Arguments:
- tokens: bfloat16 [256, 1024, 128], P('lat', 'lon'), may hold values from -40 to 40
- region1: int32 [256, 1024], P('lat', 'lon'), may hold values from 0 to 1
- region2: int32 [128, 512], P('lat', 'lon'), may hold values from 0 to 1
- bias_index: int32 [64, 64], replicated, may hold values from 0 to 224
- ln1_gain: float32 [128], replicated, may hold values from 0.1 to 1.9
- qkv_weight1: bfloat16 [128, 384], replicated, may hold values from -2.5 to 2.5
- out_weight1: bfloat16 [128, 128], replicated, may hold values from -0.5 to 0.5
- bias_table1: float32 [225, 4], replicated, may hold values from -4 to 4
- merge_gain: float32 [512], replicated, may hold values from 0.1 to 1.9
- merge_weight: bfloat16 [512, 256], replicated, may hold values from -0.25 to 0.25
- ln2_gain: float32 [256], replicated, may hold values from 0.1 to 1.9
- qkv_weight2: bfloat16 [256, 768], replicated, may hold values from -2.5 to 2.5
- out_weight2: bfloat16 [256, 256], replicated, may hold values from -0.375 to 0.375
- bias_table2: float32 [225, 8], replicated, may hold values from -4 to 4
- cot_fine: bfloat16 [256, 1024, 128], P('lat', 'lon'), may hold values from -6 to 6
- cot_coarse: bfloat16 [128, 512, 256], P('lat', 'lon'), may hold values from -6 to 6
Outputs:
- coarse_out: bfloat16 [128, 512, 256], P('lat', 'lon')
- grad_tokens: bfloat16 [256, 1024, 128], P('lat', 'lon')
- grad_ln1_gain: float32 [128], replicated
- grad_qkv1: float32 [128, 384], replicated
- grad_out1: float32 [128, 128], replicated
- grad_table1: float32 [225, 4], replicated
- grad_merge_gain: float32 [512], replicated
- grad_merge: float32 [512, 256], replicated
- grad_ln2_gain: float32 [256], replicated
- grad_qkv2: float32 [256, 768], replicated
- grad_out2: float32 [256, 256], replicated
- grad_table2: float32 [225, 8], replicated
All inputs are finite; a program needn't handle non-finite values.
Results may differ from a plain program's by a relative error of at most 0.029.
The roundings to bfloat16 on the way count: a program that leaves them out, or rounds other values in their place, can miss the bound.
Values may be sent and summed in bfloat16 or wider, within the bound.
No kernel may reach another device: no remote copies, remote signals or barrier semaphores. Data moves between devices by JAX's collectives and lax.ppermute only.
A program may use at most 64 MiB of HBM per device.

v0:
```python
from functools import partial
import math

import jax
import jax.numpy as jnp
from jax import lax
from jax.experimental import pallas as pl
from jax.experimental.pallas import tpu as pltpu
from jax.sharding import PartitionSpec as P

WIN = 8
RIM = 4
TOK = WIN * WIN
EPSILON = 1e-05
MASKED = -1000000000.0
F32 = jnp.float32
BF16 = jnp.bfloat16
LON = ("z", "yl")
LAT = ("yh", "x", "c")
CHIPS = ("z", "yl", "yh", "x")
VMEM_LIMIT = 24 * 1024 * 1024


def nt_dot(a, b):
    return lax.dot_general(a, b, (((1,), (1,)), ((), ())), preferred_element_type=F32)


def tn_dot(a, b):
    return lax.dot_general(a, b, (((0,), (0,)), ((), ())), preferred_element_type=F32)


def nn_dot(a, b):
    return jnp.dot(a, b, preferred_element_type=F32)


def head_masks():
    rows = lax.broadcasted_iota(jnp.int32, (4 * TOK, 128), 0) // TOK
    lanes = lax.broadcasted_iota(jnp.int32, (4 * TOK, 128), 1) // 32
    return rows == lanes


def spread_heads(part, hm):
    return jnp.where(hm, jnp.concatenate([part] * 4, 0), jnp.zeros((), part.dtype))


def fold_heads(wide, hm):
    kept = jnp.where(hm, wide, 0.0)
    return (kept[:TOK] + kept[TOK : 2 * TOK]) + (kept[2 * TOK : 3 * TOK] + kept[3 * TOK :])


def probs(q4, k, bias, same):
    scores = nt_dot(k, q4) * (32 ** (-0.5)) + bias
    scores = jnp.where(jnp.concatenate([same, same], 1) > 0.5, scores, MASKED)
    top = jnp.max(scores, axis=0, keepdims=True)
    grown = jnp.exp(scores - top)
    return grown * (1.0 / jnp.sum(grown, axis=0, keepdims=True))


def unit_forward(q, k, v, bias, same, hm):
    weights = probs(spread_heads(q, hm), k, bias, same).astype(BF16)
    return fold_heads(tn_dot(weights, v), hm).astype(BF16)


def unit_backward(q, k, v, g, bias, same, hm):
    q4 = spread_heads(q, hm)
    g4 = spread_heads(g, hm)
    p = probs(q4, k, bias, same)
    dp = nt_dot(v, g4).astype(BF16).astype(F32)
    ds = p * (dp - jnp.sum(p * dp, axis=0, keepdims=True))
    dsb = (ds * (32 ** (-0.5))).astype(BF16)
    dq = fold_heads(tn_dot(dsb, k), hm).astype(BF16)
    dk = nn_dot(dsb, q4).astype(BF16)
    dv = nn_dot(p.astype(BF16), g4).astype(BF16)
    return dq, dk, dv, ds


def same_keys(onehot):
    return nt_dot(onehot, jnp.concatenate([onehot] * 2, 0))


def unit_norm(x):
    centered = x - jnp.mean(x, axis=-1, keepdims=True)
    rstd = lax.rsqrt(jnp.mean(centered * centered, axis=-1, keepdims=True) + EPSILON)
    return centered * rstd, rstd


def norm_back(hat, rstd, cot, gain):
    d = cot * gain
    return rstd * (
        d - jnp.mean(d, axis=-1, keepdims=True) - hat * jnp.mean(d * hat, axis=-1, keepdims=True)
    )


def pulled(field, own, rows, cols, corner, rim, rc, cc):
    feat = field.shape[-1]
    field[0:rc, 0:cc] = own.astype(F32)
    field[rc : rc + rim, 0:cc] = rows.astype(F32).reshape(rim, cc, feat)
    field[0:rc, cc : cc + rim] = cols.astype(F32).reshape(rc, rim, feat)
    field[rc : rc + rim, cc : cc + rim] = corner.astype(F32).reshape(rim, rim, feat)


def pushed(field, own, rows, cols, corner, rim, rc, cc):
    feat = field.shape[-1]
    field[rim : rim + rc, rim : rim + cc] = own.astype(F32)
    field[0:rim, rim : rim + cc] = rows.astype(F32).reshape(rim, cc, feat)
    field[rim : rim + rc, 0:rim] = cols.astype(F32).reshape(rc, rim, feat)
    field[0:rim, 0:rim] = corner.astype(F32).reshape(rim, rim, feat)


HALF = 2048
COARSE = 1536


def other_core():
    return 1 - lax.axis_index("c")


def table_sums(totals, index, spread):
    lane = lax.broadcasted_iota(jnp.int32, (TOK // 2, 128), 1)
    spread[...] = jnp.zeros(spread.shape, F32)
    head = 0
    for total in totals:
        for p in range(2):
            block = total[:, p * 128 : (p + 1) * 128]
            upper, lower = block[: TOK // 2], block[TOK // 2 :]
            spread[:, head, :] = jnp.where(lane < 64, upper, pltpu.roll(lower, 64, 1))
            spread[:, head + 1, :] = jnp.where(lane < 64, pltpu.roll(upper, 64, 1), lower)
            head += 2
    entry = lax.broadcasted_iota(jnp.int32, (256, 256), 0)
    sums = jnp.zeros((32, 256), F32)
    for q in range(TOK // 4):
        part = jnp.concatenate([spread[2 * q], spread[2 * q + 1]], 1)
        high = part.astype(BF16)
        low = (part - high.astype(F32)).astype(BF16)
        at = jnp.concatenate([index[2 * q : 2 * q + 1, :], index[2 * q + 1 : 2 * q + 2, :]], 1)
        chosen = jnp.where(entry == at, 1.0, 0.0).astype(BF16)
        sums = sums + nt_dot(jnp.concatenate([high, low], 0), chosen)
    return sums[:16] + sums[16:]


def fetch(sources, copies, sems):
    started = [
        pltpu.make_async_copy(source, copy, sems.at[n])
        for n, (source, copy) in enumerate(zip(sources, copies))
    ]
    for one in started:
        one.start()
    for one in started:
        one.wait()


def strips_kernel(x_in, cf_in, cc2_in, x, cf, cc2, row_out, col_out, corner_out, sems):
    fetch((x_in, cf_in, cc2_in), (x, cf, cc2), sems)
    rc, cc, feat = cf.shape
    r2, c2, _ = cc2.shape
    nr, nc, nk = RIM * cc, rc * RIM, RIM * RIM
    row_out[0:nr] = x[0:RIM].reshape(nr, feat)
    cols = x[:, 0:16, :].astype(F32)[:, :RIM]
    col_out[0:nc] = cols.reshape(nc, feat).astype(BF16)
    corner_out[0:nk] = cols[:RIM].reshape(nk, feat).astype(BF16)
    row_out[nr : 3 * nr] = cf[0 : 2 * RIM].reshape(2 * nr, feat)
    cols = cf[:, 0:16, :].astype(F32)[:, : 2 * RIM]
    col_out[nc : 3 * nc] = cols.reshape(2 * nc, feat).astype(BF16)
    corner_out[nk : 5 * nk] = cols[: 2 * RIM].reshape(4 * nk, feat).astype(BF16)
    cols = cc2[:, 0:16, :].astype(F32)[:, :RIM]
    for half in range(2):
        lanes = slice(half * feat, (half + 1) * feat)
        row_out[3 * nr + half * nr // 2 : 3 * nr + (half + 1) * nr // 2] = cc2[
            0:RIM, :, lanes
        ].reshape(nr // 2, feat)
        part = cols[:, :, lanes]
        col_out[3 * nc + half * nc // 2 : 3 * nc + (half + 1) * nc // 2] = part.reshape(
            nc // 2, feat
        ).astype(BF16)
        corner_out[5 * nk + half * nk : 5 * nk + (half + 1) * nk] = (
            part[:RIM].reshape(nk, feat).astype(BF16)
        )


def prepare_kernel(kept, *refs):
    sources, refs = refs[1 : 6 + kept], refs[6 + kept :]
    copies, refs, tables, near, sems = refs[:kept], refs[kept:-7], refs[-7], refs[-6:-1], refs[-1]
    fetch(sources, near + copies, sems)
    region1, region2, index, table1, table2 = near
    keys1, keys2, bias1, bias2, pairs_out = refs
    last = lax.axis_index(LAT) == lax.axis_size(LAT) - 1
    token = lax.broadcasted_iota(jnp.int32, (TOK, 128), 0)
    lane = lax.broadcasted_iota(jnp.int32, (TOK, 128), 1)
    for region, out in ((region1, keys1), (region2, keys2)):
        rows, columns = region.shape
        labels = jnp.broadcast_to(region[...][:, :, None], (rows, columns, 128))
        w = 0
        for a in range(rows // WIN):
            for b in range(columns // WIN):
                key = 2 * labels[WIN * a : WIN * (a + 1), WIN * b : WIN * (b + 1)].reshape(TOK, 128)
                if a == rows // WIN - 1:
                    key = key + jnp.where(
                        jnp.logical_and(last, token >= RIM * WIN), 1, 0
                    )
                onehot = jnp.where(key == lane, 1.0, 0.0).astype(BF16)
                out[w * TOK : (w + 1) * TOK, :] = same_keys(onehot)
                w += 1
    tables[...] = jnp.zeros(tables.shape, F32)
    h1, entries = table1.shape
    h2 = table2.shape[0]
    tables[0:h1, 0:entries] = table1[...]
    tables[8 : 8 + h2, 0:entries] = table2[...]
    turned = index[...].T
    at = jnp.concatenate([turned, turned], 1)
    pairs_out[...] = jnp.concatenate([turned[: TOK // 2], turned[TOK // 2 :]], 1)
    small = jnp.bitwise_and(at, 127)

    def looked_up(h):
        found = [
            jnp.take_along_axis(
                jnp.broadcast_to(tables[h : h + 1, p * 128 : (p + 1) * 128], (TOK, 128)), small, axis=1
            )
            for p in range(2)
        ]
        return jnp.where(at < 128, found[0], found[1])

    for out, base, heads in ((bias1, 0, h1), (bias2, 8, h2)):
        for p in range(heads // 2):
            out[:, p * 128 : (p + 1) * 128] = jnp.where(
                lane < 64, looked_up(base + 2 * p), looked_up(base + 2 * p + 1)
            )


def cores_kernel(keep, got, out):
    out[...] = (keep[...] + got[...]).reshape(out.shape).astype(BF16)


def sum_kernel(scale, parts, out):
    total = jnp.sum(parts[...].astype(F32), axis=0) * scale
    out[...] = jnp.broadcast_to(total[None], out.shape).astype(BF16)


def unpack_kernel(own, got, gain1, qkv1, out1, table1, mgain, merge, gain2, qkv2, out2, table2, field):
    other = other_core()
    field[1 - other] = own[...].astype(F32).reshape(HALF, 128)
    field[other] = got[...].astype(F32).reshape(HALF, 128)
    feat = out1.shape[0]
    feat2 = out2.shape[0]
    for b in range(6):
        qkv2[:, b * feat : (b + 1) * feat] = field[0, b * feat2 : (b + 1) * feat2, :]
    for b in range(2):
        out2[:, b * feat : (b + 1) * feat] = field[1, b * feat2 : (b + 1) * feat2, :]
        r0 = 2 * feat2 + b * 4 * feat
        merge[:, b * feat : (b + 1) * feat] = field[1, r0 : r0 + 4 * feat, :]
    for b in range(3):
        r0 = COARSE + b * feat
        qkv1[:, b * feat : (b + 1) * feat] = field[0, r0 : r0 + feat, :]
    out1[...] = field[1, COARSE : COARSE + feat, :]
    r0 = COARSE + feat
    tables = jnp.concatenate([field[1, r0 : r0 + 16, :], field[1, r0 + 16 : r0 + 32, :]], 1)
    h1, entries = table1.shape
    h2 = table2.shape[0]
    table1[...] = tables[0:h1, 0:entries]
    table2[...] = tables[h1 : h1 + h2, 0:entries]
    gains = field[1, r0 + 32 : r0 + 40, :]
    gain1[...] = gains[0:1]
    for q in range(4):
        mgain[:, q * feat : (q + 1) * feat] = gains[1 + q : 2 + q]
    for q in range(2):
        gain2[:, q * feat : (q + 1) * feat] = gains[5 + q : 6 + q]


def fine_forward_kernel(
    x, xr, xc, xk, keys, bias, gain, wqkv, wout,
    xw_out, qkv_out, mixed_out, own_out, row_out, col_out, corner_out,
    field, grid,
):
    rc, cc, feat = x.shape
    pulled(
        field, x[...], xr[: RIM * cc], xc[: rc * RIM], xk[: RIM * RIM], RIM, rc, cc
    )
    hm = head_masks()
    wide = cc // WIN
    group = 4
    for a in range(rc // WIN):
        for b0 in range(0, wide, group):
            r0 = RIM + WIN * a
            parts = [
                field[r0 : r0 + WIN, RIM + WIN * b : RIM + WIN * (b + 1), :].reshape(TOK, feat)
                for b in range(b0, b0 + group)
            ]
            tokens = jnp.concatenate(parts, 0)
            t0 = (a * wide + b0) * TOK
            span = pl.ds(t0, group * TOK)
            xw_out[span, :] = tokens.astype(BF16)
            hat, _ = unit_norm(tokens)
            normed = (hat * gain[...]).astype(BF16)
            qkv = nn_dot(normed, wqkv[...]).astype(BF16)
            qkv_out[span, :] = qkv
            mixed = []
            for n in range(group):
                w = a * wide + b0 + n
                rows = slice(n * TOK, (n + 1) * TOK)
                mixed.append(
                    unit_forward(
                        qkv[rows, :feat],
                        qkv[rows, feat : 2 * feat],
                        qkv[rows, 2 * feat :],
                        bias[...],
                        keys[w * TOK : (w + 1) * TOK, :],
                        hm,
                    )
                )
            mixed = jnp.concatenate(mixed, 0)
            mixed_out[span, :] = mixed
            result = tokens + nn_dot(mixed, wout[...])
            for n in range(group):
                b = b0 + n
                grid[WIN * a : WIN * (a + 1), WIN * b : WIN * (b + 1), :] = result[
                    n * TOK : (n + 1) * TOK
                ].reshape(WIN, WIN, feat)
    own_out[...] = grid[...].astype(BF16)
    row_out[...] = grid[0:RIM].reshape(RIM * cc, feat).astype(BF16)
    col_out[...] = grid[:, 0:RIM].reshape(rc * RIM, feat).astype(BF16)
    corner_out[...] = grid[0:RIM, 0:RIM].reshape(RIM * RIM, feat).astype(BF16)


def coarse_kernel(
    f, fr, fc, fk, cf, cc2, cr, ccl, ck,
    keys, bias, mgain, wmerge, gain, wqkv, wout,
    own_out, fine_out, row_out, col_out, corner_out,
    packed, gmgain, ggain, gbias,
    field, cfield, coarse_field, fgrid, cgrid,
):
    rc, cc, feat = f.shape
    r2, c2 = rc // 2, cc // 2
    feat2 = 2 * feat
    wide = c2 // WIN
    windows = [(a, b) for a in range(r2 // WIN) for b in range(wide)]
    count = len(windows) * TOK
    hm = head_masks()
    pulled(field, f[...], fr[...], fc[...], fk[...], RIM, rc, cc)
    nr, nc, nk = RIM * cc, rc * RIM, RIM * RIM
    pulled(cfield, cf[...], cr[nr : 3 * nr], ccl[nc : 3 * nc], ck[nk : 5 * nk], 2 * RIM, rc, cc)
    for half in range(2):
        lanes = slice(half * feat, (half + 1) * feat)
        pulled(
            coarse_field.at[half],
            cc2[:, :, lanes],
            cr[pl.ds(3 * nr + half * nr // 2, nr // 2)],
            ccl[pl.ds(3 * nc + half * nc // 2, nc // 2)],
            ck[pl.ds(5 * nk + half * nk, nk)],
            RIM,
            r2,
            c2,
        )

    def in_windows(load):
        return jnp.concatenate([load(a, b).reshape(TOK, feat) for a, b in windows], 0)

    def joined_part(ref, rim, quad):
        dc, dr = quad // 2, quad % 2

        def load(a, b):
            return jnp.stack(
                [
                    ref[
                        rim + 2 * (WIN * a + r) + dr,
                        pl.ds(rim + 2 * WIN * b + dc, WIN, stride=2),
                        :,
                    ]
                    for r in range(WIN)
                ],
                0,
            )

        return in_windows(load)

    parts = [joined_part(field, RIM, quad) for quad in range(4)]
    mean = sum(jnp.sum(p, axis=-1, keepdims=True) for p in parts) * (1.0 / (4 * feat))
    centered = [p - mean for p in parts]
    spread = sum(jnp.sum(p * p, axis=-1, keepdims=True) for p in centered) * (1.0 / (4 * feat))
    mrstd = lax.rsqrt(spread + EPSILON)
    mhat = [p * mrstd for p in centered]
    mgains = [mgain[:, q * feat : (q + 1) * feat] for q in range(4)]
    mnormed = jnp.concatenate([(h * g).astype(BF16) for h, g in zip(mhat, mgains)], 1)
    coarse_in = nn_dot(mnormed, wmerge[...]).astype(BF16).astype(F32)
    hat, rstd = unit_norm(coarse_in)
    normed = (hat * gain[...]).astype(BF16)
    qkv = nn_dot(normed, wqkv[...]).astype(BF16)
    mixed = []
    for w in range(len(windows)):
        rows = slice(w * TOK, (w + 1) * TOK)
        units = []
        same = keys[rows, :]
        for g in range(2):
            lo = g * feat
            units.append(
                unit_forward(
                    qkv[rows, lo : lo + feat],
                    qkv[rows, feat2 + lo : feat2 + lo + feat],
                    qkv[rows, 2 * feat2 + lo : 2 * feat2 + lo + feat],
                    bias[:, g * 4 * TOK : (g + 1) * 4 * TOK],
                    same,
                    hm,
                )
            )
        mixed.append(jnp.concatenate(units, 1))
    mixed = jnp.concatenate(mixed, 0)
    result = coarse_in + nn_dot(mixed, wout[...])
    for w, (a, b) in enumerate(windows):
        for half in range(2):
            cgrid[half, WIN * a : WIN * (a + 1), WIN * b : WIN * (b + 1), :] = result[
                w * TOK : (w + 1) * TOK, half * feat : (half + 1) * feat
            ].reshape(WIN, WIN, feat)
    cot = jnp.concatenate(
        [
            in_windows(
                lambda a, b: coarse_field[
                    half,
                    RIM + WIN * a : RIM + WIN * (a + 1),
                    RIM + WIN * b : RIM + WIN * (b + 1),
                    :,
                ]
            )
            for half in range(2)
        ],
        1,
    )
    cotb = cot.astype(BF16)
    grad = tn_dot(mixed, cotb)
    for b in range(2):
        packed[1, b * feat2 : (b + 1) * feat2, :] = grad[:, b * feat : (b + 1) * feat]
    cot_mixed = nt_dot(cotb, wout[...]).astype(BF16)
    cot_rows = []
    total = [jnp.zeros((TOK, 4 * TOK), F32) for _ in range(2)]
    for w in range(len(windows)):
        rows = slice(w * TOK, (w + 1) * TOK)
        dqs, dks, dvs = [], [], []
        same = keys[rows, :]
        for g in range(2):
            lo = g * feat
            dq, dk, dv, ds = unit_backward(
                qkv[rows, lo : lo + feat],
                qkv[rows, feat2 + lo : feat2 + lo + feat],
                qkv[rows, 2 * feat2 + lo : 2 * feat2 + lo + feat],
                cot_mixed[rows, lo : lo + feat],
                bias[:, g * 4 * TOK : (g + 1) * 4 * TOK],
                same,
                hm,
            )
            dqs.append(dq)
            dks.append(dk)
            dvs.append(dv)
            total[g] = total[g] + ds
        cot_rows.append(jnp.concatenate(dqs + dks + dvs, 1))
    gbias[...] = jnp.concatenate(total, 1)
    cot_qkv = jnp.concatenate(cot_rows, 0)
    grad = tn_dot(normed, cot_qkv)
    for b in range(6):
        packed[0, b * feat2 : (b + 1) * feat2, :] = grad[:, b * feat : (b + 1) * feat]
    cot_unit = nt_dot(cot_qkv, wqkv[...]).astype(BF16).astype(F32)
    ggain[...] = jnp.sum(cot_unit * hat, axis=0, keepdims=True)
    cot_in = (cot + norm_back(hat, rstd, cot_unit, gain[...])).astype(BF16)
    grad = tn_dot(mnormed, cot_in)
    for b in range(2):
        r0 = 2 * feat2 + b * 4 * feat
        packed[1, r0 : r0 + 4 * feat, :] = grad[:, b * feat : (b + 1) * feat]
    cot_norm = nt_dot(cot_in, wmerge[...]).astype(BF16).astype(F32)
    cot_parts = [cot_norm[:, q * feat : (q + 1) * feat] for q in range(4)]
    gmgain[...] = jnp.concatenate(
        [jnp.sum(c * h, axis=0, keepdims=True) for c, h in zip(cot_parts, mhat)], 1
    )
    ds = [c * g for c, g in zip(cot_parts, mgains)]
    mean_d = sum(jnp.sum(d, axis=-1, keepdims=True) for d in ds) * (1.0 / (4 * feat))
    mean_dh = sum(jnp.sum(d * h, axis=-1, keepdims=True) for d, h in zip(ds, mhat)) * (
        1.0 / (4 * feat)
    )
    for quad in range(4):
        dc, dr = quad // 2, quad % 2
        back = mrstd * (ds[quad] - mean_d - mhat[quad] * mean_dh)
        back = back + joined_part(cfield, 2 * RIM, quad)
        for w, (a, b) in enumerate(windows):
            for r in range(WIN):
                t0 = w * TOK + r * WIN
                fgrid[
                    2 * (WIN * a + r) + dr, pl.ds(2 * WIN * b + dc, WIN, stride=2), :
                ] = back[t0 : t0 + WIN]
    own_out[...] = cgrid[...].astype(BF16)
    fine_out[...] = fgrid[...].astype(BF16)
    row_out[...] = fgrid[rc - RIM :].reshape(nr, feat).astype(BF16)
    col_out[...] = fgrid[:, cc - RIM :].reshape(nc, feat).astype(BF16)
    corner_out[...] = fgrid[rc - RIM :, cc - RIM :].reshape(nk, feat).astype(BF16)


def fine_backward_kernel(
    c, d, er, ec, ek, xw, qkv_in, mixed_in, keys, bias, gain, wqkv, wout,
    gmgain, ggain2, gbias2, index, coarse_grads,
    own_out, row_out, col_out, corner_out, send_out, keep_out,
    field, grid, packed, spread,
):
    rc, cc, feat = c.shape
    r2, c2 = rc // 2, cc // 2
    nr, nc, nk = RIM * cc, rc * RIM, RIM * RIM
    pushed(field, c[...], er[...], ec[...], ek[...], RIM, rc, cc)
    hm = head_masks()
    wide = cc // WIN
    group = 4
    total = jnp.zeros((TOK, 4 * TOK), F32)
    total_gain = jnp.zeros((1, feat), F32)
    total_out = jnp.zeros((feat, feat), F32)
    total_qkv = jnp.zeros((feat, 3 * feat), F32)
    for a in range(rc // WIN):
        for b0 in range(0, wide, group):
            cot = jnp.concatenate(
                [
                    field[
                        WIN * a : WIN * (a + 1), WIN * b : WIN * (b + 1), :
                    ].reshape(TOK, feat)
                    for b in range(b0, b0 + group)
                ],
                0,
            )
            t0 = (a * wide + b0) * TOK
            span = pl.ds(t0, group * TOK)
            cotb = cot.astype(BF16)
            total_out = total_out + tn_dot(mixed_in[span, :], cotb)
            cot_mixed = nt_dot(cotb, wout[...]).astype(BF16)
            qkv = qkv_in[span, :]
            cot_rows = []
            for n in range(group):
                w = a * wide + b0 + n
                rows = slice(n * TOK, (n + 1) * TOK)
                dq, dk, dv, ds = unit_backward(
                    qkv[rows, :feat],
                    qkv[rows, feat : 2 * feat],
                    qkv[rows, 2 * feat :],
                    cot_mixed[rows],
                    bias[...],
                    keys[w * TOK : (w + 1) * TOK, :],
                    hm,
                )
                total = total + ds
                cot_rows.append(jnp.concatenate([dq, dk, dv], 1))
            cot_qkv = jnp.concatenate(cot_rows, 0)
            hat, rstd = unit_norm(xw[span, :].astype(F32))
            normed = (hat * gain[...]).astype(BF16)
            total_qkv = total_qkv + tn_dot(normed, cot_qkv)
            cot_unit = nt_dot(cot_qkv, wqkv[...]).astype(BF16).astype(F32)
            total_gain = total_gain + jnp.sum(cot_unit * hat, axis=0, keepdims=True)
            result = cot + norm_back(hat, rstd, cot_unit, gain[...])
            for n in range(group):
                b = b0 + n
                grid[WIN * a : WIN * (a + 1), WIN * b : WIN * (b + 1), :] = result[
                    n * TOK : (n + 1) * TOK
                ].reshape(WIN, WIN, feat)
    for b in range(3):
        packed[0, b * feat : (b + 1) * feat, :] = total_qkv[:, b * feat : (b + 1) * feat]
    packed[0, 3 * feat :, :] = jnp.zeros((feat, feat), F32)
    packed[1, 0:feat, :] = total_out
    tables = table_sums([total, gbias2[:, : 4 * TOK], gbias2[:, 4 * TOK :]], index, spread)
    packed[1, feat : feat + 16, :] = tables[:, :feat]
    packed[1, feat + 16 : feat + 32, :] = tables[:, feat:]
    gains = jnp.concatenate(
        [total_gain]
        + [gmgain[:, q * feat : (q + 1) * feat] for q in range(4)]
        + [ggain2[:, q * feat : (q + 1) * feat] for q in range(2)]
        + [jnp.zeros((1, feat), F32)],
        0,
    )
    packed[1, feat + 32 : feat + 40, :] = gains
    packed[1, feat + 40 :, :] = jnp.zeros((3 * feat - 40, feat), F32)
    other = other_core()
    send_out[0:COARSE, :] = coarse_grads[other]
    send_out[COARSE:HALF, :] = packed[other]
    keep_out[0:COARSE, :] = coarse_grads[1 - other]
    keep_out[COARSE:HALF, :] = packed[1 - other]
    own_out[...] = grid[...].astype(BF16)
    row_out[0:nr] = grid[rc - RIM :].reshape(nr, feat).astype(BF16)
    col_out[0:nc] = grid[:, cc - RIM :].reshape(nc, feat).astype(BF16)
    corner_out[0:nk] = grid[rc - RIM :, cc - RIM :].reshape(nk, feat).astype(BF16)
    coarse = d[...].astype(F32)
    for half in range(2):
        row_out[nr + half * nr // 2 : nr + (half + 1) * nr // 2] = (
            coarse[half, r2 - RIM :].reshape(nr // 2, feat).astype(BF16)
        )
        col_out[nc + half * nc // 2 : nc + (half + 1) * nc // 2] = (
            coarse[half, :, c2 - RIM :].reshape(nc // 2, feat).astype(BF16)
        )
        corner_out[nk + half * nk : nk + (half + 1) * nk] = (
            coarse[half, r2 - RIM :, c2 - RIM :].reshape(nk, feat).astype(BF16)
        )


def place_kernel(c, d, er, ec, ek, out, coarse_out, field, dfield):
    rc, cc, feat = c.shape
    r2, c2 = rc // 2, cc // 2
    nr, nc, nk = RIM * cc, rc * RIM, RIM * RIM
    pushed(field, c[...], er[0:nr], ec[0:nc], ek[0:nk], RIM, rc, cc)
    out[...] = field[0:rc, 0:cc].astype(BF16)
    for half in range(2):
        pushed(
            dfield.at[half],
            d[half],
            er[pl.ds(nr + half * nr // 2, nr // 2)],
            ec[pl.ds(nc + half * nc // 2, nc // 2)],
            ek[pl.ds(nk + half * nk, nk)],
            RIM,
            r2,
            c2,
        )
        coarse_out[:, :, half * feat : (half + 1) * feat] = dfield[half, 0:r2, 0:c2].astype(BF16)


def call(kernel, outs, scratch, *args):
    return pl.pallas_call(
        kernel,
        name=getattr(kernel, "func", kernel).__name__,
        out_shape=outs,
        scratch_shapes=[pltpu.VMEM(s, F32) for s in scratch],
        compiler_params=pltpu.CompilerParams(vmem_limit_bytes=VMEM_LIMIT),
    )(*args)


def sds(*shape, dtype=BF16):
    return jax.ShapeDtypeStruct(shape, dtype)


def send(rows, cols, corner, sense):
    nlat, nlon = lax.axis_size(LAT), lax.axis_size(LON)
    lat = [(i, (i + sense) % nlat) for i in range(nlat)]
    lon = [(i, (i + sense) % nlon) for i in range(nlon)]
    both = [
        (j * nlat + i, (j + sense) % nlon * nlat + (i + sense) % nlat)
        for i in range(nlat)
        for j in range(nlon)
    ]
    return (
        lax.ppermute(rows, LAT, lat),
        lax.ppermute(cols, LON, lon),
        lax.ppermute(corner, LON + LAT, both),
    )


def along_torus(values):
    return lax.all_to_all(values, CHIPS, 0, 0, tiled=False)


def per_device(
    tokens, region1, region2, bias_index, ln1_gain, qkv_weight1, out_weight1, bias_table1,
    merge_gain, merge_weight, ln2_gain, qkv_weight2, out_weight2, bias_table2, cot_fine, cot_coarse,
):
    rc, cc, feat = tokens.shape
    r2, c2, feat2 = cot_coarse.shape
    heads1, heads2 = bias_table1.shape[1], bias_table2.shape[1]
    entries = bias_table1.shape[0]
    n_tok = rc * cc
    nr, nc, nk = RIM * cc, rc * RIM, RIM * RIM
    f32 = partial(sds, dtype=F32)

    near = partial(pltpu.with_memory_space_constraint, memory_space=pltpu.HBM)
    far = pl.BlockSpec(memory_space=pltpu.HBM)
    params = pltpu.CompilerParams(vmem_limit_bytes=VMEM_LIMIT)
    fields = (tokens, cot_fine, cot_coarse)
    *fields, row, col, corner = pl.pallas_call(
        strips_kernel,
        out_shape=[sds(*v.shape) for v in fields]
        + [sds(4 * nr, feat), sds(4 * nc, feat), sds(7 * nk, feat)],
        in_specs=[far] * 3,
        scratch_shapes=[pltpu.SemaphoreType.DMA((3,))],
        compiler_params=params,
        name="strips",
    )(*[near(v) for v in fields])
    tokens, cot_fine, cot_coarse = fields
    small = (region1, region2, bias_index, bias_table1.T, bias_table2.T)
    kept = (
        ln1_gain.reshape(1, feat), ln2_gain.reshape(1, feat2), merge_gain.reshape(1, 4 * feat),
        qkv_weight1, out_weight1, merge_weight, qkv_weight2, out_weight2,
    )
    gain1, gain2, mgain, wqkv1, wout1, wmerge, wqkv2, wout2, keys1, keys2, bias1, bias2, pairs = pl.pallas_call(
        partial(prepare_kernel, len(kept)),
        out_shape=[sds(*v.shape, dtype=v.dtype) for v in kept]
        + [
            f32(n_tok, 128), f32(n_tok // 4, 128), f32(TOK, heads1 * TOK), f32(TOK, heads2 * TOK),
            sds(TOK // 2, 2 * TOK, dtype=jnp.int32),
        ],
        in_specs=[pl.BlockSpec(memory_space=pltpu.VMEM)] + [far] * (len(small) + len(kept)),
        scratch_shapes=[pltpu.VMEM((16, 256), F32)]
        + [pltpu.VMEM(v.shape, v.dtype) for v in small]
        + [pltpu.SemaphoreType.DMA((len(small) + len(kept),))],
        compiler_params=params,
        name="prepare",
    )(corner, *[near(v) for v in small + kept])
    row, col, corner = send(row, col, corner, -1)
    xw, qkv, mixed, fs, fr, fc, fk = call(
        fine_forward_kernel,
        (
            sds(n_tok, feat), sds(n_tok, 3 * feat), sds(n_tok, feat), sds(rc, cc, feat),
            sds(nr, feat), sds(nc, feat), sds(nk, feat),
        ),
        [(rc + RIM, cc + 2 * RIM, feat), (rc, cc, feat)],
        tokens, row, col, corner, keys1, bias1, gain1, wqkv1, wout1,
    )
    fr, fc, fk = send(fr, fc, fk, -1)
    cs, cfo, er, ec, ek, coarse_grads, gmgain, ggain2, gbias2 = call(
        coarse_kernel,
        (
            sds(2, r2, c2, feat), sds(rc, cc, feat), sds(nr, feat), sds(nc, feat), sds(nk, feat),
            f32(2, COARSE, feat), f32(1, 4 * feat), f32(1, feat2), f32(TOK, heads2 * TOK),
        ),
        [
            (rc + RIM, cc + 2 * RIM, feat), (rc + 2 * RIM, cc + 2 * RIM, feat),
            (2, r2 + RIM, c2 + 2 * RIM, feat), (rc, cc, feat), (2, r2, c2, feat),
        ],
        fs, fr, fc, fk, cot_fine, cot_coarse, row, col, corner,
        keys2, bias2, mgain, wmerge, gain2, wqkv2, wout2,
    )
    er, ec, ek = send(er, ec, ek, 1)
    back, br, bc, bk, sent, held = call(
        fine_backward_kernel,
        (
            sds(rc, cc, feat), sds(2 * nr, feat), sds(2 * nc, feat), sds(3 * nk, feat),
            f32(HALF, feat), f32(HALF, feat),
        ),
        [
            (rc + RIM, cc + 2 * RIM, feat), (rc, cc, feat), (2, HALF - COARSE, feat), (TOK // 2, 16, 128),
        ],
        cfo, cs, er, ec, ek, xw, qkv, mixed, keys1, bias1, gain1, wqkv1, wout1,
        gmgain, ggain2, gbias2, pairs, coarse_grads,
    )
    br, bc, bk = send(br, bc, bk, 1)
    got = lax.ppermute(sent, "c", [(0, 1), (1, 0)])
    chips = math.prod(lax.axis_size(a) for a in CHIPS)
    blocks = sds(chips, HALF // chips, feat)
    parts = along_torus(call(cores_kernel, blocks, [], held, got))
    scale = 4.0 / math.sqrt(n_tok * chips * lax.axis_size("c"))
    part = call(partial(sum_kernel, scale), blocks, [], parts)
    part, br, bc, bk = lax.optimization_barrier((part, br, bc, bk))
    part = along_torus(part)
    grad_tokens, coarse_out = call(
        place_kernel,
        (sds(rc, cc, feat), sds(r2, c2, feat2)),
        [(rc + RIM, cc + 2 * RIM, feat), (2, r2 + RIM, c2 + 2 * RIM, feat)],
        back, cs, br, bc, bk,
    )
    g = call(
        unpack_kernel,
        (
            f32(1, feat), f32(feat, 3 * feat), f32(feat, feat), f32(heads1, entries),
            f32(1, 4 * feat), f32(4 * feat, feat2), f32(1, feat2), f32(feat2, 3 * feat2),
            f32(feat2, feat2), f32(heads2, entries),
        ),
        [(2, HALF, feat)],
        part, lax.ppermute(part, "c", [(0, 1), (1, 0)]),
    )
    return (
        coarse_out, grad_tokens, g[0].reshape(-1), g[1], g[2], g[3].T, g[4].reshape(-1), g[5],
        g[6].reshape(-1), g[7], g[8], g[9].T,
    )


def solution(mesh):
    fine_mesh = jax.sharding.Mesh(
        mesh.devices.reshape(8, 2, 2, 4, 2), ("z", "yl", "yh", "x", "c")
    )
    grid = P(LAT, LON, None)
    flat = P(LAT, LON)
    return jax.shard_map(
        per_device,
        mesh=fine_mesh,
        in_specs=(grid, flat, flat) + (P(),) * 11 + (grid, grid),
        out_specs=(grid, grid) + (P(),) * 10,
        check_vma=False,
    )
```

profile of v0, /device:TPU:1, one launch (start us, length us, event | category | flops | bytes accessed | tf_op | source)
XLA Modules:
  0.0 112.9 jit_solution(17471195564455619033)
XLA Ops:
  0.6 1.1 %strips.1 = (bf16[16,64,128]{2,1,0:T(8,128)(2,1)S(1)}, bf16[16,64,128]{2,1,0:T(8,128)(2,1)S(1)}, bf16[8,32,256]{2,1,0:T(8,128)(2,1)S(1)}, bf16[1024,128]{1,0:T(8...) custom-call(bf16[16,64,128]{2,1,0:T(8,128)(2,1)} %x_in.1, bf16[16,64,128]{2,1,0:T(8,128)(2,1)} %cf_in.1, ...), custom_call_target="tpu_custom_call" | custom-call | tf_op jit(solution)/shard_map/strips/pallas_call | solution.py:660
  1.8 3.3 %collective-permute-start = (bf16[1024,128]{1,0:T(8,128)(2,1)S(1)}, bf16[1024,128]{1,0:T(8,128)(2,1)S(1)}, u32[]{:S(2)}, u32[]{:S(2)}) collective-permute-start(bf16[1024,128]{1,0:T(8,128)(2,1)S(1)} %get-tuple-element.70), channel_id=1, source_target_pairs={{0,15},{1,0},{2,1},{3,2},{4,3},{5,4},{6,5},{7,6},{8,7},{9,8},{10,9... | collective-permute-start | bytes 786440 | tf_op jit(solution)/shard_map/ppermute | solution.py:634
  5.1 4.9 %collective-permute-start.1 = (bf16[256,128]{1,0:T(8,128)(2,1)S(1)}, bf16[256,128]{1,0:T(8,128)(2,1)S(1)}, u32[]{:S(2)}, u32[]{:S(2)}) collective-permute-start(bf16[256,128]{1,0:T(8,128)(2,1)S(1)} %get-tuple-element.71), channel_id=1, source_target_pairs={{0,240},{16,0},{32,16},{48,32},{64,48},{80,64},{96,80},{112,96},{1... | collective-permute-start | bytes 196616 | tf_op jit(solution)/shard_map/ppermute | solution.py:635
  10.0 5.2 %collective-permute-start.2 = (bf16[112,128]{1,0:T(8,128)(2,1)S(1)}, bf16[112,128]{1,0:T(8,128)(2,1)S(1)}, u32[]{:S(2)}, u32[]{:S(2)}) collective-permute-start(bf16[112,128]{1,0:T(8,128)(2,1)S(1)} %get-tuple-element.72.refs_0_), channel_id=1, source_target_pairs={{0,255},{16,15},{32,31},{48,47},{64,63},{80,79},{96,95},{112,111},... | collective-permute-start | bytes 86024 | tf_op jit(solution)/shard_map/ppermute | solution.py:636
  15.1 2.5 %prepare.1 = (f32[1,128]{1,0:T(1,128)S(1)}, f32[1,256]{1,0:T(1,128)S(1)}, f32[1,512]{1,0:T(1,128)S(1)}, bf16[128,384]{1,0:T(8,128)(2,1)S(1)}, bf16[128,128]{1,0:...) custom-call(bf16[112,128]{1,0:T(8,128)(2,1)S(1)} %get-tuple-element., ...), custom_call_target="tpu_custom_call" | custom-call | tf_op jit(solution)/shard_map/prepare/pallas_call | solution.py:675
  17.6 0.0 collective-permute-done.2.xk.ck
  17.6 0.0 collective-permute-done.1.xc.ccl
  17.6 0.0 collective-permute-done.xr.cr
  17.6 3.4 %fine_forward_kernel.1 = (bf16[1024,128]{1,0:T(8,128)(2,1)S(1)}, bf16[1024,384]{1,0:T(8,128)(2,1)S(1)}, bf16[1024,128]{1,0:T(8,128)(2,1)S(1)}, bf16[16,64,128]{2...) custom-call(bf16[16,64,128]{2,1,0:T(8,128)(2,1)S(1)} %get-tuple-eleme, ...), custom_call_target="tpu_custom_call" | custom-call | tf_op jit(solution)/shard_map/fine_forward_kernel/pallas_call | solution.py:611
  21.1 0.1 collective-permute-start.3
  21.2 3.2 %collective-permute-start.4 = (bf16[64,128]{1,0:T(8,128)(2,1)S(1)}, bf16[64,128]{1,0:T(8,128)(2,1)S(1)}, u32[]{:S(2)}, u32[]{:S(2)}) collective-permute-start(bf16[64,128]{1,0:T(8,128)(2,1)S(1)} %get-tuple-element.80), channel_id=1, source_target_pairs={{0,240},{16,0},{32,16},{48,32},{64,48},{80,64},{96,80},{112,96},{1... | collective-permute-start | bytes 49160 | tf_op jit(solution)/shard_map/ppermute | solution.py:635
  24.4 4.1 %collective-permute-start.5 = (bf16[16,128]{1,0:T(8,128)(2,1)S(1)}, bf16[16,128]{1,0:T(8,128)(2,1)S(1)}, u32[]{:S(2)}, u32[]{:S(2)}) collective-permute-start(bf16[16,128]{1,0:T(8,128)(2,1)S(1)} %get-tuple-element.81), channel_id=1, source_target_pairs={{0,255},{16,15},{32,31},{48,47},{64,63},{80,79},{96,95},{112,111},... | collective-permute-start | bytes 12296 | tf_op jit(solution)/shard_map/ppermute | solution.py:636
  28.5 0.8 collective-permute-done.5.fk
  29.3 0.0 collective-permute-done.4.fc
  29.3 0.0 collective-permute-done.3.fr
  29.3 4.7 %coarse_kernel.1 = (bf16[2,8,32,128]{3,2,1,0:T(8,128)(2,1)S(1)}, bf16[16,64,128]{2,1,0:T(8,128)(2,1)S(1)}, bf16[256,128]{1,0:T(8,128)(2,1)S(1)}, bf16[64,128]{1,...) custom-call(bf16[16,64,128]{2,1,0:T(8,128)(2,1)S(1)} %get-tuple-elem, ...), custom_call_target="tpu_custom_call" | custom-call | tf_op jit(solution)/shard_map/coarse_kernel/pallas_call | solution.py:611
  34.0 0.1 collective-permute-start.6
  34.1 1.3 %collective-permute-start.7 = (bf16[64,128]{1,0:T(8,128)(2,1)S(1)}, bf16[64,128]{1,0:T(8,128)(2,1)S(1)}, u32[]{:S(2)}, u32[]{:S(2)}) collective-permute-start(bf16[64,128]{1,0:T(8,128)(2,1)S(1)} %get-tuple-element.94), channel_id=1, source_target_pairs={{0,16},{16,32},{32,48},{48,64},{64,80},{80,96},{96,112},{112,128},... | collective-permute-start | bytes 49160 | tf_op jit(solution)/shard_map/ppermute | solution.py:635
  35.4 0.0 collective-permute-start.8
  35.4 6.4 %collective-permute-done.8.ek = bf16[16,128]{1,0:T(8,128)(2,1)S(1)} collective-permute-done((bf16[16,128]{1,0:T(8,128)(2,1)S(1)}, bf16[16,128]{1,0:T(8,128)(2,1)S(1)}, u32[]{:S(2)}, u32[]{:S(2)}) %collective-permute-start.8) | collective-permute-done | bytes 4128 | tf_op jit(solution)/shard_map/ppermute | solution.py:636
  41.8 0.0 collective-permute-done.7.ec
  41.8 0.0 collective-permute-done.6.er
  41.8 7.0 %fine_backward_kernel.1 = (bf16[16,64,128]{2,1,0:T(8,128)(2,1)S(1)}, bf16[512,128]{1,0:T(8,128)(2,1)S(1)}, bf16[128,128]{1,0:T(8,128)(2,1)S(1)}, bf16[48,128]{1,...) custom-call(bf16[16,64,128]{2,1,0:T(8,128)(2,1)S(1)} %get-tuple-element.91.c, ...), custom_call_target="tpu_custom_call" | custom-call | tf_op jit(solution)/shard_map/fine_backward_kernel/pallas_call | solution.py:611
  48.8 3.5 %collective-permute-start.9 = (f32[2048,128]{1,0:T(8,128)S(1)}, f32[2048,128]{1,0:T(8,128)S(1)}, u32[]{:S(2)}, u32[]{:S(2)}) collective-permute-start(f32[2048,128]{1,0:T(8,128)S(1)} %get-tuple-element.106), channel_id=1, source_target_pairs={{0,1},{1,0},{2,3},{3,2},{4,5},{5,4},{6,7},{7,6},{8,9},{9,8},{10,11... | collective-permute-start | bytes 3145736 | tf_op jit(solution)/shard_map/ppermute | solution.py:727
  52.3 2.3 %collective-permute-done.9.got = f32[2048,128]{1,0:T(8,128)S(1)} collective-permute-done((f32[2048,128]{1,0:T(8,128)S(1)}, f32[2048,128]{1,0:T(8,128)S(1)}, u32[]{:S(2)}, u32[]{:S(2)}) %collective-permute-start.9) | collective-permute-done | bytes 1048608 | tf_op jit(solution)/shard_map/ppermute | solution.py:727
  54.6 1.0 cores_kernel.1
  55.6 7.8 %all-to-all-start = ((bf16[128,16,128]{2,1,0:T(8,128)(2,1)}), bf16[128,16,128]{2,1,0:T(8,128)(2,1)S(1)}, u32[]{:S(2)}, u32[]{:S(2)}) async-start(bf16[128,16,128]{2,1,0:T(8,128)(2,1)} %cores_kernel.1), calls=%async_computation | async-start | bytes 1048576 | tf_op jit(solution)/shard_map/all_to_all | solution.py:641
  63.4 1.2 %collective-permute-start.10 = (bf16[512,128]{1,0:T(8,128)(2,1)S(1)}, bf16[512,128]{1,0:T(8,128)(2,1)S(1)}, u32[]{:S(2)}, u32[]{:S(2)}) collective-permute-start(bf16[512,128]{1,0:T(8,128)(2,1)S(1)} %get-tuple-element.107), channel_id=1, source_target_pairs={{0,1},{1,2},{2,3},{3,4},{4,5},{5,6},{6,7},{7,8},{8,9},{9,10},{10,1... | collective-permute-start | bytes 393224 | tf_op jit(solution)/shard_map/ppermute | solution.py:634
  64.7 1.2 %collective-permute-start.11 = (bf16[128,128]{1,0:T(8,128)(2,1)S(1)}, bf16[128,128]{1,0:T(8,128)(2,1)S(1)}, u32[]{:S(2)}, u32[]{:S(2)}) collective-permute-start(bf16[128,128]{1,0:T(8,128)(2,1)S(1)} %get-tuple-element.108), channel_id=1, source_target_pairs={{0,16},{16,32},{32,48},{48,64},{64,80},{80,96},{96,112},{112,128},... | collective-permute-start | bytes 98312 | tf_op jit(solution)/shard_map/ppermute | solution.py:635
  65.9 1.3 %collective-permute-start.12 = (bf16[48,128]{1,0:T(8,128)(2,1)S(1)}, bf16[48,128]{1,0:T(8,128)(2,1)S(1)}, u32[]{:S(2)}, u32[]{:S(2)}) collective-permute-start(bf16[48,128]{1,0:T(8,128)(2,1)S(1)} %get-tuple-element.109), channel_id=1, source_target_pairs={{0,17},{16,33},{32,49},{48,65},{64,81},{80,97},{96,113},{112,129},... | collective-permute-start | bytes 36872 | tf_op jit(solution)/shard_map/ppermute | solution.py:636
  67.1 14.1 %all-to-all-done.parts = bf16[128,16,128]{2,1,0:T(8,128)(2,1)S(1)} async-done(((bf16[128,16,128]{2,1,0:T(8,128)(2,1)}), bf16[128,16,128]{2,1,0:T(8,128)(2,1)S(1)}, u32[]{:S(2)}, u32[]{:S(2)}) %all-to-all-start) | async-done | bytes 524320 | tf_op jit(solution)/shard_map/all_to_all | solution.py:641
  81.3 0.2 sum_kernel.1
  81.4 0.0 collective-permute-done.12.ek
  81.4 0.0 collective-permute-done.11.ec
  81.5 0.0 collective-permute-done.10.er
  81.5 25.6 %all_to_all.10.own = bf16[128,16,128]{2,1,0:T(8,128)(2,1)S(1)} all-to-all(bf16[128,16,128]{2,1,0:T(8,128)(2,1)S(1)} %sum_kernel.1), channel_id=1, replica_groups=mesh['z'=8,'yl'=2,'yh'=2,'x'=4,'c'=2] {'z','yl','yh','x'}, dimensions={0} | all-to-all | bytes 1048576 | tf_op jit(solution)/shard_map/all_to_all | solution.py:641
  107.0 3.0 %collective-permute-start.13 = (bf16[128,16,128]{2,1,0:T(8,128)(2,1)S(1)}, bf16[128,16,128]{2,1,0:T(8,128)(2,1)S(1)}, u32[]{:S(2)}, u32[]{:S(2)}) collective-permute-start(bf16[128,16,128]{2,1,0:T(8,128)(2,1)S(1)} %all_to_all.10.own), channel_id=1, source_target_pairs={{0,1},{1,0},{2,3},{3,2},{4,5},{5,4},{6,7},{7,6},{8,9},{9,8},{10,11... | collective-permute-start | bytes 1572872 | tf_op jit(solution)/shard_map/ppermute | solution.py:749
  110.0 0.8 place_kernel.1
  110.9 0.7 collective-permute-done.13.got
  111.6 1.3 %unpack_kernel.1 = (f32[1,128]{1,0:T(1,128)}, f32[128,384]{1,0:T(8,128)}, f32[128,128]{1,0:T(8,128)}, f32[4,225]{1,0:T(4,128)}, f32[1,512]{1,0:T(1,128)}, /*inde...) custom-call(bf16[128,16,128]{2,1,0:T(8,128)(2,1)S(1)} %all_to_all.10.own, ...), custom_call_target="tpu_custom_call" | custom-call | tf_op jit(solution)/shard_map/unpack_kernel/pallas_call | solution.py:611
Async XLA Ops:
  1.8 15.8 %collective-permute-start = (bf16[1024,128]{1,0:T(8,128)(2,1)S(1)}, bf16[1024,128]{1,0:T(8,128)(2,1)S(1)}, u32[]{:S(2)}, u32[]{:S(2)}) collective-permute-start(bf16[1024,128]{1,0:T(8,128)(2,1)S(1)} %get-tuple-element.70), channel_id=1, source_target_pairs={{0,15},{1,0},{2,1},{3,2},{4,3},{5,4},{6,5},{7,6},{8,7},{9,8},{10,9... | collective-permute-start | bytes 786440 | tf_op jit(solution)/shard_map/ppermute | solution.py:634
  5.1 12.5 %collective-permute-start.1 = (bf16[256,128]{1,0:T(8,128)(2,1)S(1)}, bf16[256,128]{1,0:T(8,128)(2,1)S(1)}, u32[]{:S(2)}, u32[]{:S(2)}) collective-permute-start(bf16[256,128]{1,0:T(8,128)(2,1)S(1)} %get-tuple-element.71), channel_id=1, source_target_pairs={{0,240},{16,0},{32,16},{48,32},{64,48},{80,64},{96,80},{112,96},{1... | collective-permute-start | bytes 196616 | tf_op jit(solution)/shard_map/ppermute | solution.py:635
  10.0 7.6 %collective-permute-start.2 = (bf16[112,128]{1,0:T(8,128)(2,1)S(1)}, bf16[112,128]{1,0:T(8,128)(2,1)S(1)}, u32[]{:S(2)}, u32[]{:S(2)}) collective-permute-start(bf16[112,128]{1,0:T(8,128)(2,1)S(1)} %get-tuple-element.72.refs_0_), channel_id=1, source_target_pairs={{0,255},{16,15},{32,31},{48,47},{64,63},{80,79},{96,95},{112,111},... | collective-permute-start | bytes 86024 | tf_op jit(solution)/shard_map/ppermute | solution.py:636
  21.1 8.2 %collective-permute-start.3 = (bf16[256,128]{1,0:T(8,128)(2,1)S(1)}, bf16[256,128]{1,0:T(8,128)(2,1)S(1)}, u32[]{:S(2)}, u32[]{:S(2)}) collective-permute-start(bf16[256,128]{1,0:T(8,128)(2,1)S(1)} %get-tuple-element.79), channel_id=1, source_target_pairs={{0,15},{1,0},{2,1},{3,2},{4,3},{5,4},{6,5},{7,6},{8,7},{9,8},{10,9... | collective-permute-start | bytes 196616 | tf_op jit(solution)/shard_map/ppermute | solution.py:634
  21.2 8.1 %collective-permute-start.4 = (bf16[64,128]{1,0:T(8,128)(2,1)S(1)}, bf16[64,128]{1,0:T(8,128)(2,1)S(1)}, u32[]{:S(2)}, u32[]{:S(2)}) collective-permute-start(bf16[64,128]{1,0:T(8,128)(2,1)S(1)} %get-tuple-element.80), channel_id=1, source_target_pairs={{0,240},{16,0},{32,16},{48,32},{64,48},{80,64},{96,80},{112,96},{1... | collective-permute-start | bytes 49160 | tf_op jit(solution)/shard_map/ppermute | solution.py:635
  24.4 4.9 %collective-permute-start.5 = (bf16[16,128]{1,0:T(8,128)(2,1)S(1)}, bf16[16,128]{1,0:T(8,128)(2,1)S(1)}, u32[]{:S(2)}, u32[]{:S(2)}) collective-permute-start(bf16[16,128]{1,0:T(8,128)(2,1)S(1)} %get-tuple-element.81), channel_id=1, source_target_pairs={{0,255},{16,15},{32,31},{48,47},{64,63},{80,79},{96,95},{112,111},... | collective-permute-start | bytes 12296 | tf_op jit(solution)/shard_map/ppermute | solution.py:636
  34.0 7.8 %collective-permute-start.6 = (bf16[256,128]{1,0:T(8,128)(2,1)S(1)}, bf16[256,128]{1,0:T(8,128)(2,1)S(1)}, u32[]{:S(2)}, u32[]{:S(2)}) collective-permute-start(bf16[256,128]{1,0:T(8,128)(2,1)S(1)} %get-tuple-element.93), channel_id=1, source_target_pairs={{0,1},{1,2},{2,3},{3,4},{4,5},{5,6},{6,7},{7,8},{8,9},{9,10},{10,1... | collective-permute-start | bytes 196616 | tf_op jit(solution)/shard_map/ppermute | solution.py:634
  34.1 7.7 %collective-permute-start.7 = (bf16[64,128]{1,0:T(8,128)(2,1)S(1)}, bf16[64,128]{1,0:T(8,128)(2,1)S(1)}, u32[]{:S(2)}, u32[]{:S(2)}) collective-permute-start(bf16[64,128]{1,0:T(8,128)(2,1)S(1)} %get-tuple-element.94), channel_id=1, source_target_pairs={{0,16},{16,32},{32,48},{48,64},{64,80},{80,96},{96,112},{112,128},... | collective-permute-start | bytes 49160 | tf_op jit(solution)/shard_map/ppermute | solution.py:635
  35.4 6.4 %collective-permute-start.8 = (bf16[16,128]{1,0:T(8,128)(2,1)S(1)}, bf16[16,128]{1,0:T(8,128)(2,1)S(1)}, u32[]{:S(2)}, u32[]{:S(2)}) collective-permute-start(bf16[16,128]{1,0:T(8,128)(2,1)S(1)} %get-tuple-element.95), channel_id=1, source_target_pairs={{0,17},{16,33},{32,49},{48,65},{64,81},{80,97},{96,113},{112,129},... | collective-permute-start | bytes 12296 | tf_op jit(solution)/shard_map/ppermute | solution.py:636
  48.8 5.8 %collective-permute-start.9 = (f32[2048,128]{1,0:T(8,128)S(1)}, f32[2048,128]{1,0:T(8,128)S(1)}, u32[]{:S(2)}, u32[]{:S(2)}) collective-permute-start(f32[2048,128]{1,0:T(8,128)S(1)} %get-tuple-element.106), channel_id=1, source_target_pairs={{0,1},{1,0},{2,3},{3,2},{4,5},{5,4},{6,7},{7,6},{8,9},{9,8},{10,11... | collective-permute-start | bytes 3145736 | tf_op jit(solution)/shard_map/ppermute | solution.py:727
  55.6 25.7 %all-to-all-start = ((bf16[128,16,128]{2,1,0:T(8,128)(2,1)}), bf16[128,16,128]{2,1,0:T(8,128)(2,1)S(1)}, u32[]{:S(2)}, u32[]{:S(2)}) async-start(bf16[128,16,128]{2,1,0:T(8,128)(2,1)} %cores_kernel.1), calls=%async_computation | async-start | bytes 1048576 | tf_op jit(solution)/shard_map/all_to_all | solution.py:641
  63.4 18.0 %collective-permute-start.10 = (bf16[512,128]{1,0:T(8,128)(2,1)S(1)}, bf16[512,128]{1,0:T(8,128)(2,1)S(1)}, u32[]{:S(2)}, u32[]{:S(2)}) collective-permute-start(bf16[512,128]{1,0:T(8,128)(2,1)S(1)} %get-tuple-element.107), channel_id=1, source_target_pairs={{0,1},{1,2},{2,3},{3,4},{4,5},{5,6},{6,7},{7,8},{8,9},{9,10},{10,1... | collective-permute-start | bytes 393224 | tf_op jit(solution)/shard_map/ppermute | solution.py:634
  64.7 16.8 %collective-permute-start.11 = (bf16[128,128]{1,0:T(8,128)(2,1)S(1)}, bf16[128,128]{1,0:T(8,128)(2,1)S(1)}, u32[]{:S(2)}, u32[]{:S(2)}) collective-permute-start(bf16[128,128]{1,0:T(8,128)(2,1)S(1)} %get-tuple-element.108), channel_id=1, source_target_pairs={{0,16},{16,32},{32,48},{48,64},{64,80},{80,96},{96,112},{112,128},... | collective-permute-start | bytes 98312 | tf_op jit(solution)/shard_map/ppermute | solution.py:635
  65.9 15.6 %collective-permute-start.12 = (bf16[48,128]{1,0:T(8,128)(2,1)S(1)}, bf16[48,128]{1,0:T(8,128)(2,1)S(1)}, u32[]{:S(2)}, u32[]{:S(2)}) collective-permute-start(bf16[48,128]{1,0:T(8,128)(2,1)S(1)} %get-tuple-element.109), channel_id=1, source_target_pairs={{0,17},{16,33},{32,49},{48,65},{64,81},{80,97},{96,113},{112,129},... | collective-permute-start | bytes 36872 | tf_op jit(solution)/shard_map/ppermute | solution.py:636
  107.0 4.6 %collective-permute-start.13 = (bf16[128,16,128]{2,1,0:T(8,128)(2,1)S(1)}, bf16[128,16,128]{2,1,0:T(8,128)(2,1)S(1)}, u32[]{:S(2)}, u32[]{:S(2)}) collective-permute-start(bf16[128,16,128]{2,1,0:T(8,128)(2,1)S(1)} %all_to_all.10.own), channel_id=1, source_target_pairs={{0,1},{1,0},{2,3},{3,2},{4,5},{5,4},{6,7},{7,6},{8,9},{9,8},{10,11... | collective-permute-start | bytes 1572872 | tf_op jit(solution)/shard_map/ppermute | solution.py:749
where the time goes:
time: 113 us
  starting transfers between devices  40.3 us (36%)
  blocking collectives  25.6 us (23%)
  waiting for transfers between devices  24.3 us (22%)
  Pallas kernels  22 us (19%)
    all_to_all x1, blocking collectives, along_torus(): return lax.all_to_all(values, CHIPS, 0, 0, tiled=False)  25.6 us
    pallas_call x7, Pallas kernels, call(): pl.pallas_call(kernel, name=getattr(kernel, 'func', kernel).__name__, out...  18.4 us
    all_to_all x1, waiting for transfers between devices, along_torus(): return lax.all_to_all(values, CHIPS, 0, 0, tiled=False)  14.1 us
    ppermute x4, starting transfers between devices, send(): lax.ppermute(corner, LON + LAT, both)  10.6 us
    ppermute x4, starting transfers between devices, send(): lax.ppermute(cols, LON, lon)  10.6 us
    all_to_all x1, starting transfers between devices, along_torus(): return lax.all_to_all(values, CHIPS, 0, 0, tiled=False)  7.84 us
    ppermute x4, waiting for transfers between devices, send(): lax.ppermute(corner, LON + LAT, both)  7.14 us
    ppermute x4, starting transfers between devices, send(): lax.ppermute(rows, LAT, lat)  4.72 us
  transfers between devices with their start and end apart: 15, of which 5 were waited for; matrix products, arithmetic and copies ran while one was open for 0% of the time, Pallas kernels for 3%

commit v1 on v0

--- a/solution.py
+++ b/solution.py
@@ -18,6 +18,9 @@
 LON = ("z", "yl")
 LAT = ("yh", "x", "c")
 CHIPS = ("z", "yl", "yh", "x")
+EXTRA_ROWS = 12
+EXTRA_COLS = 16
+LABELS = 16
 VMEM_LIMIT = 24 * 1024 * 1024
 
 
@@ -39,43 +42,70 @@
     return rows == lanes
 
 
-def spread_heads(part, hm):
-    return jnp.where(hm, jnp.concatenate([part] * 4, 0), jnp.zeros((), part.dtype))
-
-
-def fold_heads(wide, hm):
-    kept = jnp.where(hm, wide, 0.0)
-    return (kept[:TOK] + kept[TOK : 2 * TOK]) + (kept[2 * TOK : 3 * TOK] + kept[3 * TOK :])
-
-
-def probs(q4, k, bias, same):
-    scores = nt_dot(k, q4) * (32 ** (-0.5)) + bias
-    scores = jnp.where(jnp.concatenate([same, same], 1) > 0.5, scores, MASKED)
-    top = jnp.max(scores, axis=0, keepdims=True)
+def spread_heads(pair, hm):
+    return jnp.concatenate(
+        [jnp.where(hm, jnp.concatenate([p] * 4, 0), jnp.zeros((), p.dtype)) for p in pair], 1
+    )
+
+
+def diagonal(pair):
+    zero = jnp.zeros(pair[0].shape, pair[0].dtype)
+    return jnp.concatenate(
+        [jnp.concatenate([pair[0], zero], 1), jnp.concatenate([zero, pair[1]], 1)], 0
+    )
+
+
+def fold_heads(wide):
+    head = lax.broadcasted_iota(jnp.int32, (TOK, 128), 1) // 32
+    return jnp.where(
+        head < 2,
+        jnp.where(head < 1, wide[:TOK], wide[TOK : 2 * TOK]),
+        jnp.where(head < 3, wide[2 * TOK : 3 * TOK], wide[3 * TOK :]),
+    )
+
+
+def by_query(weights, pair):
+    turned = jnp.concatenate([weights[h] for h in range(4)], 1).T
+    out = []
+    for w in range(2):
+        rows = jnp.concatenate(
+            [turned[(2 * h + w) * TOK : (2 * h + w + 1) * TOK] for h in range(4)], 0
+        )
+        out.append(fold_heads(nn_dot(rows, pair[w])).astype(BF16))
+    return out
+
+
+def by_key(weights, spread):
+    wide = nn_dot(weights.reshape(4 * TOK, 2 * TOK), spread)
+    return [fold_heads(wide[:, w * 128 : (w + 1) * 128]).astype(BF16) for w in range(2)]
+
+
+def probs(k4, q2, bias, same):
+    scores = nt_dot(k4, q2).reshape(4, TOK, 2 * TOK) * (32 ** (-0.5)) + bias
+    scores = jnp.where(same[None] > 0.5, scores, MASKED)
+    top = jnp.max(scores, axis=1, keepdims=True)
     grown = jnp.exp(scores - top)
-    return grown * (1.0 / jnp.sum(grown, axis=0, keepdims=True))
+    return grown * (1.0 / jnp.sum(grown, axis=1, keepdims=True))
 
 
 def unit_forward(q, k, v, bias, same, hm):
-    weights = probs(spread_heads(q, hm), k, bias, same).astype(BF16)
-    return fold_heads(tn_dot(weights, v), hm).astype(BF16)
+    weights = probs(spread_heads(k, hm), diagonal(q), bias, same).astype(BF16)
+    return by_query(weights, v)
 
 
 def unit_backward(q, k, v, g, bias, same, hm):
-    q4 = spread_heads(q, hm)
-    g4 = spread_heads(g, hm)
-    p = probs(q4, k, bias, same)
-    dp = nt_dot(v, g4).astype(BF16).astype(F32)
-    ds = p * (dp - jnp.sum(p * dp, axis=0, keepdims=True))
+    q2, g2 = diagonal(q), diagonal(g)
+    p = probs(spread_heads(k, hm), q2, bias, same)
+    dp = nt_dot(spread_heads(v, hm), g2).astype(BF16).astype(F32).reshape(p.shape)
+    ds = p * (dp - jnp.sum(p * dp, axis=1, keepdims=True))
     dsb = (ds * (32 ** (-0.5))).astype(BF16)
-    dq = fold_heads(tn_dot(dsb, k), hm).astype(BF16)
-    dk = nn_dot(dsb, q4).astype(BF16)
-    dv = nn_dot(p.astype(BF16), g4).astype(BF16)
-    return dq, dk, dv, ds
-
-
-def same_keys(onehot):
-    return nt_dot(onehot, jnp.concatenate([onehot] * 2, 0))
+    return by_query(dsb, k), by_key(dsb, q2), by_key(p.astype(BF16), g2), ds
+
+
+def same_keys(first, second):
+    both = jnp.concatenate([first, second], 0)
+    lane = lax.broadcasted_iota(jnp.int32, (TOK, 2 * TOK), 1)
+    return jnp.where(lane < TOK, nt_dot(first, both), nt_dot(second, both))
 
 
 def unit_norm(x):
@@ -109,6 +139,7 @@
 
 HALF = 2048
 COARSE = 1536
+SMALL = 40
 
 
 def other_core():
@@ -120,12 +151,10 @@
     spread[...] = jnp.zeros(spread.shape, F32)
     head = 0
     for total in totals:
-        for p in range(2):
-            block = total[:, p * 128 : (p + 1) * 128]
-            upper, lower = block[: TOK // 2], block[TOK // 2 :]
-            spread[:, head, :] = jnp.where(lane < 64, upper, pltpu.roll(lower, 64, 1))
-            spread[:, head + 1, :] = jnp.where(lane < 64, pltpu.roll(upper, 64, 1), lower)
-            head += 2
+        for h in range(4):
+            block = total[h] + pltpu.roll(total[h], TOK, 1)
+            spread[:, head, :] = jnp.where(lane < TOK, block[: TOK // 2], block[TOK // 2 :])
+            head += 1
     entry = lax.broadcasted_iota(jnp.int32, (256, 256), 0)
     sums = jnp.zeros((32, 256), F32)
     for q in range(TOK // 4):
@@ -149,32 +178,40 @@
         one.wait()
 
 
-def strips_kernel(x_in, cf_in, cc2_in, x, cf, cc2, row_out, col_out, corner_out, sems):
-    fetch((x_in, cf_in, cc2_in), (x, cf, cc2), sems)
+def strip_sizes(rc, cc):
+    nr, nc, nk = RIM * cc, rc * RIM, RIM * RIM
+    row = EXTRA_ROWS * cc, 2 * nr, nr, LABELS
+    col = rc * EXTRA_COLS, 2 * nc, nc, LABELS
+    corner = EXTRA_ROWS * EXTRA_COLS, 4 * nk, 2 * nk, LABELS
+    return [[sum(sizes[: n + 1]) for n in range(4)] for sizes in (row, col, corner)]
+
+
+def strips_kernel(x_in, cf_in, cc2_in, region_in, x, cf, cc2, row_out, col_out, corner_out, region, labels, sems):
+    fetch((x_in, cf_in, cc2_in, region_in), (x, cf, cc2, region), sems)
     rc, cc, feat = cf.shape
     r2, c2, _ = cc2.shape
     nr, nc, nk = RIM * cc, rc * RIM, RIM * RIM
-    row_out[0:nr] = x[0:RIM].reshape(nr, feat)
-    cols = x[:, 0:16, :].astype(F32)[:, :RIM]
-    col_out[0:nc] = cols.reshape(nc, feat).astype(BF16)
-    corner_out[0:nk] = cols[:RIM].reshape(nk, feat).astype(BF16)
-    row_out[nr : 3 * nr] = cf[0 : 2 * RIM].reshape(2 * nr, feat)
+    row, col, corner = strip_sizes(rc, cc)
+    row_out[0 : row[0]] = x[0:EXTRA_ROWS].reshape(row[0], feat)
+    cols = x[:, 0:EXTRA_COLS, :]
+    col_out[0 : col[0]] = cols.reshape(col[0], feat)
+    corner_out[0 : corner[0]] = cols[:EXTRA_ROWS].reshape(corner[0], feat)
+    row_out[row[0] : row[1]] = cf[0 : 2 * RIM].reshape(2 * nr, feat)
     cols = cf[:, 0:16, :].astype(F32)[:, : 2 * RIM]
-    col_out[nc : 3 * nc] = cols.reshape(2 * nc, feat).astype(BF16)
-    corner_out[nk : 5 * nk] = cols[: 2 * RIM].reshape(4 * nk, feat).astype(BF16)
+    col_out[col[0] : col[1]] = cols.reshape(2 * nc, feat).astype(BF16)
+    corner_out[corner[0] : corner[1]] = cols[: 2 * RIM].reshape(4 * nk, feat).astype(BF16)
     cols = cc2[:, 0:16, :].astype(F32)[:, :RIM]
     for half in range(2):
         lanes = slice(half * feat, (half + 1) * feat)
-        row_out[3 * nr + half * nr // 2 : 3 * nr + (half + 1) * nr // 2] = cc2[
-            0:RIM, :, lanes
-        ].reshape(nr // 2, feat)
+        r0, c0, k0 = row[1] + half * nr // 2, col[1] + half * nc // 2, corner[1] + half * nk
+        row_out[r0 : r0 + nr // 2] = cc2[0:RIM, :, lanes].reshape(nr // 2, feat)
         part = cols[:, :, lanes]
-        col_out[3 * nc + half * nc // 2 : 3 * nc + (half + 1) * nc // 2] = part.reshape(
-            nc // 2, feat
-        ).astype(BF16)
-        corner_out[5 * nk + half * nk : 5 * nk + (half + 1) * nk] = (
-            part[:RIM].reshape(nk, feat).astype(BF16)
-        )
+        col_out[c0 : c0 + nc // 2] = part.reshape(nc // 2, feat).astype(BF16)
+        corner_out[k0 : k0 + nk] = part[:RIM].reshape(nk, feat).astype(BF16)
+    labels[...] = jnp.zeros(labels.shape, F32)
+    labels[0:rc, 0:cc] = region[...].astype(F32)
+    for out, ends in ((row_out, row), (col_out, col), (corner_out, corner)):
+        out[ends[2] : ends[3]] = labels[...].astype(BF16)
 
 
 def prepare_kernel(kept, *refs):
@@ -189,17 +226,15 @@
     for region, out in ((region1, keys1), (region2, keys2)):
         rows, columns = region.shape
         labels = jnp.broadcast_to(region[...][:, :, None], (rows, columns, 128))
-        w = 0
+        onehots = []
         for a in range(rows // WIN):
             for b in range(columns // WIN):
                 key = 2 * labels[WIN * a : WIN * (a + 1), WIN * b : WIN * (b + 1)].reshape(TOK, 128)
                 if a == rows // WIN - 1:
-                    key = key + jnp.where(
-                        jnp.logical_and(last, token >= RIM * WIN), 1, 0
-                    )
-                onehot = jnp.where(key == lane, 1.0, 0.0).astype(BF16)
-                out[w * TOK : (w + 1) * TOK, :] = same_keys(onehot)
-                w += 1
+                    key = key + jnp.where(jnp.logical_and(last, token >= RIM * WIN), 1, 0)
+                onehots.append(jnp.where(key == lane, 1.0, 0.0).astype(BF16))
+        for p in range(len(onehots) // 2):
+            out[p * TOK : (p + 1) * TOK, :] = same_keys(onehots[2 * p], onehots[2 * p + 1])
     tables[...] = jnp.zeros(tables.shape, F32)
     h1, entries = table1.shape
     h2 = table2.shape[0]
@@ -220,14 +255,18 @@
         return jnp.where(at < 128, found[0], found[1])
 
     for out, base, heads in ((bias1, 0, h1), (bias2, 8, h2)):
-        for p in range(heads // 2):
-            out[:, p * 128 : (p + 1) * 128] = jnp.where(
-                lane < 64, looked_up(base + 2 * p), looked_up(base + 2 * p + 1)
-            )
+        for h in range(heads):
+            out[h] = looked_up(base + h)
 
 
 def cores_kernel(keep, got, out):
-    out[...] = (keep[...] + got[...]).reshape(out.shape).astype(BF16)
+    total = keep[...] + got[...]
+    small = total[HALF - 128 : HALF - 128 + SMALL]
+    rest = small - small.astype(BF16).astype(F32)
+    total = jnp.concatenate(
+        [total[: HALF - 128], small, rest, jnp.zeros((128 - 2 * SMALL, 128), F32)], 0
+    )
+    out[...] = total.reshape(out.shape).astype(BF16)
 
 
 def sum_kernel(scale, parts, out):
@@ -251,13 +290,14 @@
         r0 = COARSE + b * feat
         qkv1[:, b * feat : (b + 1) * feat] = field[0, r0 : r0 + feat, :]
     out1[...] = field[1, COARSE : COARSE + feat, :]
-    r0 = COARSE + feat
-    tables = jnp.concatenate([field[1, r0 : r0 + 16, :], field[1, r0 + 16 : r0 + 32, :]], 1)
+    r0 = HALF - 128
+    small = field[1, r0 : r0 + SMALL, :] + field[1, r0 + SMALL : r0 + 2 * SMALL, :]
+    tables = jnp.concatenate([small[0:16], small[16:32]], 1)
     h1, entries = table1.shape
     h2 = table2.shape[0]
     table1[...] = tables[0:h1, 0:entries]
     table2[...] = tables[h1 : h1 + h2, 0:entries]
-    gains = field[1, r0 + 32 : r0 + 40, :]
+    gains = small[32:SMALL]
     gain1[...] = gains[0:1]
     for q in range(4):
         mgain[:, q * feat : (q + 1) * feat] = gains[1 + q : 2 + q]
@@ -267,61 +307,85 @@
 
 def fine_forward_kernel(
     x, xr, xc, xk, keys, bias, gain, wqkv, wout,
-    xw_out, qkv_out, mixed_out, own_out, row_out, col_out, corner_out,
+    xw_out, qkv_out, mixed_out, out,
     field, grid,
 ):
     rc, cc, feat = x.shape
-    pulled(
-        field, x[...], xr[: RIM * cc], xc[: rc * RIM], xk[: RIM * RIM], RIM, rc, cc
-    )
+    rows, cols = rc // WIN, cc // WIN
+    row, col, corner = strip_sizes(rc, cc)
+    field[0:rc, 0:cc] = x[...].astype(F32)
+    field[rc:, 0:cc] = xr[: row[0]].astype(F32).reshape(EXTRA_ROWS, cc, feat)
+    field[0:rc, cc:] = xc[: col[0]].astype(F32).reshape(rc, EXTRA_COLS, feat)
+    field[rc:, cc:] = xk[: corner[0]].astype(F32).reshape(EXTRA_ROWS, EXTRA_COLS, feat)
     hm = head_masks()
-    wide = cc // WIN
+    token = lax.broadcasted_iota(jnp.int32, (TOK, 128), 0)
+    lane = lax.broadcasted_iota(jnp.int32, (TOK, 128), 1).astype(F32)
+    last = lax.axis_index(LAT) == lax.axis_size(LAT) - 1
+    below = xr[row[2] : row[3]].astype(F32)[:WIN, :cc]
+    beside = xc[col[2] : col[3]].astype(F32)[:rc, :WIN]
+    across = xk[corner[2] : corner[3]].astype(F32)[:WIN, :WIN]
+    below = jnp.broadcast_to(below[:, :, None], (WIN, cc, 128))
+    beside = jnp.broadcast_to(beside[:, :, None], (rc, WIN, 128))
+    across = jnp.broadcast_to(across[:, :, None], (WIN, WIN, 128))
+
+    def onehot(a, b):
+        if a < rows:
+            key = 2.0 * beside[WIN * a : WIN * (a + 1)].reshape(TOK, 128)
+            if a == rows - 1:
+                key = key + jnp.where(jnp.logical_and(last, token >= RIM * WIN), 1.0, 0.0)
+        elif b < cols:
+            key = 2.0 * below[:, WIN * b : WIN * (b + 1)].reshape(TOK, 128)
+        else:
+            key = 2.0 * across.reshape(TOK, 128)
+        return jnp.where(key == lane, 1.0, 0.0).astype(BF16)
+
+    own = [(a, b) for a in range(rows) for b in range(cols)]
+    more = [(a, cols) for a in range(rows)] + [(rows, b) for b in range(cols + 1)]
+    more = more + more[-1:] * (len(more) % 2)
     group = 4
-    for a in range(rc // WIN):
-        for b0 in range(0, wide, group):
-            r0 = RIM + WIN * a
-            parts = [
-                field[r0 : r0 + WIN, RIM + WIN * b : RIM + WIN * (b + 1), :].reshape(TOK, feat)
-                for b in range(b0, b0 + group)
-            ]
-            tokens = jnp.concatenate(parts, 0)
-            t0 = (a * wide + b0) * TOK
-            span = pl.ds(t0, group * TOK)
-            xw_out[span, :] = tokens.astype(BF16)
+    for windows in (own, more):
+        for n0 in range(0, len(windows), group):
+            now = windows[n0 : n0 + group]
+            tokens = jnp.concatenate(
+                [
+                    field[
+                        RIM + WIN * a : RIM + WIN * (a + 1), RIM + WIN * b : RIM + WIN * (b + 1), :
+                    ].reshape(TOK, feat)
+                    for a, b in now
+                ],
+                0,
+            )
             hat, _ = unit_norm(tokens)
             normed = (hat * gain[...]).astype(BF16)
             qkv = nn_dot(normed, wqkv[...]).astype(BF16)
-            qkv_out[span, :] = qkv
             mixed = []
-            for n in range(group):
-                w = a * wide + b0 + n
-                rows = slice(n * TOK, (n + 1) * TOK)
-                mixed.append(
-                    unit_forward(
-                        qkv[rows, :feat],
-                        qkv[rows, feat : 2 * feat],
-                        qkv[rows, 2 * feat :],
-                        bias[...],
-                        keys[w * TOK : (w + 1) * TOK, :],
-                        hm,
-                    )
-                )
+            for n in range(0, len(now), 2):
+                parts = [
+                    [qkv[m * TOK : (m + 1) * TOK, i * feat : (i + 1) * feat] for m in (n, n + 1)]
+                    for i in range(3)
+                ]
+                if windows is own:
+                    pair = (n0 + n) // 2
+                    same = keys[pair * TOK : (pair + 1) * TOK, :]
+                else:
+                    same = same_keys(onehot(*now[n]), onehot(*now[n + 1]))
+                mixed += unit_forward(*parts, bias[...], same, hm)
             mixed = jnp.concatenate(mixed, 0)
-            mixed_out[span, :] = mixed
+            if windows is own:
+                span = pl.ds(n0 * TOK, group * TOK)
+                xw_out[span, :] = tokens.astype(BF16)
+                qkv_out[span, :] = qkv
+                mixed_out[span, :] = mixed
             result = tokens + nn_dot(mixed, wout[...])
-            for n in range(group):
-                b = b0 + n
+            for n, (a, b) in enumerate(now):
                 grid[WIN * a : WIN * (a + 1), WIN * b : WIN * (b + 1), :] = result[
                     n * TOK : (n + 1) * TOK
                 ].reshape(WIN, WIN, feat)
-    own_out[...] = grid[...].astype(BF16)
-    row_out[...] = grid[0:RIM].reshape(RIM * cc, feat).astype(BF16)
-    col_out[...] = grid[:, 0:RIM].reshape(rc * RIM, feat).astype(BF16)
-    corner_out[...] = grid[0:RIM, 0:RIM].reshape(RIM * RIM, feat).astype(BF16)
+    out[...] = grid[RIM : RIM + rc, RIM : RIM + cc, :].astype(BF16)
 
 
 def coarse_kernel(
-    f, fr, fc, fk, cf, cc2, cr, ccl, ck,
+    f, cf, cc2, cr, ccl, ck,
     keys, bias, mgain, wmerge, gain, wqkv, wout,
     own_out, fine_out, row_out, col_out, corner_out,
     packed, gmgain, ggain, gbias,
@@ -334,17 +398,26 @@
     windows = [(a, b) for a in range(r2 // WIN) for b in range(wide)]
     count = len(windows) * TOK
     hm = head_masks()
-    pulled(field, f[...], fr[...], fc[...], fk[...], RIM, rc, cc)
+    field[...] = f[...].astype(F32)
     nr, nc, nk = RIM * cc, rc * RIM, RIM * RIM
-    pulled(cfield, cf[...], cr[nr : 3 * nr], ccl[nc : 3 * nc], ck[nk : 5 * nk], 2 * RIM, rc, cc)
+    row, col, corner = strip_sizes(rc, cc)
+    pulled(
+        cfield,
+        cf[...],
+        cr[row[0] : row[1]],
+        ccl[col[0] : col[1]],
+        ck[corner[0] : corner[1]],
+        2 * RIM,
+        rc,
+        cc,
+    )
     for half in range(2):
-        lanes = slice(half * feat, (half + 1) * feat)
         pulled(
             coarse_field.at[half],
-            cc2[:, :, lanes],
-            cr[pl.ds(3 * nr + half * nr // 2, nr // 2)],
-            ccl[pl.ds(3 * nc + half * nc // 2, nc // 2)],
-            ck[pl.ds(5 * nk + half * nk, nk)],
+            cc2[:, :, half * feat : (half + 1) * feat],
+            cr[pl.ds(row[1] + half * nr // 2, nr // 2)],
+            ccl[pl.ds(col[1] + half * nc // 2, nc // 2)],
+            ck[pl.ds(corner[1] + half * nk, nk)],
             RIM,
             r2,
             c2,
@@ -371,7 +444,7 @@
 
         return in_windows(load)
 
-    parts = [joined_part(field, RIM, quad) for quad in range(4)]
+    parts = [joined_part(field, 0, quad) for quad in range(4)]
     mean = sum(jnp.sum(p, axis=-1, keepdims=True) for p in parts) * (1.0 / (4 * feat))
     centered = [p - mean for p in parts]
     spread = sum(jnp.sum(p * p, axis=-1, keepdims=True) for p in centered) * (1.0 / (4 * feat))
@@ -383,24 +456,20 @@
     hat, rstd = unit_norm(coarse_in)
     normed = (hat * gain[...]).astype(BF16)
     qkv = nn_dot(normed, wqkv[...]).astype(BF16)
+    def parts_of(wide, w, i, g):
+        lo = i * feat2 + g * feat
+        return [wide[m * TOK : (m + 1) * TOK, lo : lo + feat] for m in (w, w + 1)]
+
     mixed = []
-    for w in range(len(windows)):
-        rows = slice(w * TOK, (w + 1) * TOK)
-        units = []
-        same = keys[rows, :]
-        for g in range(2):
-            lo = g * feat
-            units.append(
-                unit_forward(
-                    qkv[rows, lo : lo + feat],
-                    qkv[rows, feat2 + lo : feat2 + lo + feat],
-                    qkv[rows, 2 * feat2 + lo : 2 * feat2 + lo + feat],
-                    bias[:, g * 4 * TOK : (g + 1) * 4 * TOK],
-                    same,
-                    hm,
-                )
+    for w in range(0, len(windows), 2):
+        same = keys[w // 2 * TOK : (w // 2 + 1) * TOK, :]
+        units = [
+            unit_forward(
+                *[parts_of(qkv, w, i, g) for i in range(3)], bias[4 * g : 4 * g + 4], same, hm
             )
-        mixed.append(jnp.concatenate(units, 1))
+            for g in range(2)
+        ]
+        mixed += [jnp.concatenate([units[0][m], units[1][m]], 1) for m in range(2)]
     mixed = jnp.concatenate(mixed, 0)
     result = coarse_in + nn_dot(mixed, wout[...])
     for w, (a, b) in enumerate(windows):
@@ -428,28 +497,26 @@
         packed[1, b * feat2 : (b + 1) * feat2, :] = grad[:, b * feat : (b + 1) * feat]
     cot_mixed = nt_dot(cotb, wout[...]).astype(BF16)
     cot_rows = []
-    total = [jnp.zeros((TOK, 4 * TOK), F32) for _ in range(2)]
-    for w in range(len(windows)):
-        rows = slice(w * TOK, (w + 1) * TOK)
-        dqs, dks, dvs = [], [], []
-        same = keys[rows, :]
+    total = [0.0, 0.0]
+    for w in range(0, len(windows), 2):
+        same = keys[w // 2 * TOK : (w // 2 + 1) * TOK, :]
+        found = []
         for g in range(2):
-            lo = g * feat
             dq, dk, dv, ds = unit_backward(
-                qkv[rows, lo : lo + feat],
-                qkv[rows, feat2 + lo : feat2 + lo + feat],
-                qkv[rows, 2 * feat2 + lo : 2 * feat2 + lo + feat],
-                cot_mixed[rows, lo : lo + feat],
-                bias[:, g * 4 * TOK : (g + 1) * 4 * TOK],
+                *[parts_of(qkv, w, i, g) for i in range(3)],
+                parts_of(cot_mixed, w, 0, g),
+                bias[4 * g : 4 * g + 4],
                 same,
                 hm,
             )
-            dqs.append(dq)
-            dks.append(dk)
-            dvs.append(dv)
+            found.append((dq, dk, dv))
             total[g] = total[g] + ds
-        cot_rows.append(jnp.concatenate(dqs + dks + dvs, 1))
-    gbias[...] = jnp.concatenate(total, 1)
+        for m in range(2):
+            cot_rows.append(
+                jnp.concatenate([found[g][i][m] for i in range(3) for g in range(2)], 1)
+            )
+    for g in range(2):
+        gbias[4 * g : 4 * g + 4] = total[g]
     cot_qkv = jnp.concatenate(cot_rows, 0)
     grad = tn_dot(normed, cot_qkv)
     for b in range(6):
@@ -501,7 +568,7 @@
     hm = head_masks()
     wide = cc // WIN
     group = 4
-    total = jnp.zeros((TOK, 4 * TOK), F32)
+    total = jnp.zeros((4, TOK, 2 * TOK), F32)
     total_gain = jnp.zeros((1, feat), F32)
     total_out = jnp.zeros((feat, feat), F32)
     total_qkv = jnp.zeros((feat, 3 * feat), F32)
@@ -523,20 +590,21 @@
             cot_mixed = nt_dot(cotb, wout[...]).astype(BF16)
             qkv = qkv_in[span, :]
             cot_rows = []
-            for n in range(group):
-                w = a * wide + b0 + n
-                rows = slice(n * TOK, (n + 1) * TOK)
+            for n in range(0, group, 2):
+                pair = (a * wide + b0 + n) // 2
+                parts = [
+                    [qkv[m * TOK : (m + 1) * TOK, i * feat : (i + 1) * feat] for m in (n, n + 1)]
+                    for i in range(3)
+                ]
                 dq, dk, dv, ds = unit_backward(
-                    qkv[rows, :feat],
-                    qkv[rows, feat : 2 * feat],
-                    qkv[rows, 2 * feat :],
-                    cot_mixed[rows],
+                    *parts,
+                    [cot_mixed[m * TOK : (m + 1) * TOK] for m in (n, n + 1)],
                     bias[...],
-                    keys[w * TOK : (w + 1) * TOK, :],
+                    keys[pair * TOK : (pair + 1) * TOK, :],
                     hm,
                 )
                 total = total + ds
-                cot_rows.append(jnp.concatenate([dq, dk, dv], 1))
+                cot_rows += [jnp.concatenate([dq[m], dk[m], dv[m]], 1) for m in range(2)]
             cot_qkv = jnp.concatenate(cot_rows, 0)
             hat, rstd = unit_norm(xw[span, :].astype(F32))
             normed = (hat * gain[...]).astype(BF16)
@@ -553,9 +621,11 @@
         packed[0, b * feat : (b + 1) * feat, :] = total_qkv[:, b * feat : (b + 1) * feat]
     packed[0, 3 * feat :, :] = jnp.zeros((feat, feat), F32)
     packed[1, 0:feat, :] = total_out
-    tables = table_sums([total, gbias2[:, : 4 * TOK], gbias2[:, 4 * TOK :]], index, spread)
-    packed[1, feat : feat + 16, :] = tables[:, :feat]
-    packed[1, feat + 16 : feat + 32, :] = tables[:, feat:]
+    tables = table_sums([total, gbias2[0:4], gbias2[4:8]], index, spread)
+    packed[1, feat : 3 * feat, :] = jnp.zeros((2 * feat, feat), F32)
+    r0 = 3 * feat
+    packed[1, r0 : r0 + 16, :] = tables[:, :feat]
+    packed[1, r0 + 16 : r0 + 32, :] = tables[:, feat:]
     gains = jnp.concatenate(
         [total_gain]
         + [gmgain[:, q * feat : (q + 1) * feat] for q in range(4)]
@@ -563,8 +633,8 @@
         + [jnp.zeros((1, feat), F32)],
         0,
     )
-    packed[1, feat + 32 : feat + 40, :] = gains
-    packed[1, feat + 40 :, :] = jnp.zeros((3 * feat - 40, feat), F32)
+    packed[1, r0 + 32 : r0 + SMALL, :] = gains
+    packed[1, r0 + SMALL :, :] = jnp.zeros((feat - SMALL, feat), F32)
     other = other_core()
     send_out[0:COARSE, :] = coarse_grads[other]
     send_out[COARSE:HALF, :] = packed[other]
@@ -660,12 +730,16 @@
     *fields, row, col, corner = pl.pallas_call(
         strips_kernel,
         out_shape=[sds(*v.shape) for v in fields]
-        + [sds(4 * nr, feat), sds(4 * nc, feat), sds(7 * nk, feat)],
-        in_specs=[far] * 3,
-        scratch_shapes=[pltpu.SemaphoreType.DMA((3,))],
+        + [sds(ends[-1], feat) for ends in strip_sizes(rc, cc)],
+        in_specs=[far] * 4,
+        scratch_shapes=[
+            pltpu.VMEM(region1.shape, region1.dtype),
+            pltpu.VMEM((LABELS, 128), F32),
+            pltpu.SemaphoreType.DMA((4,)),
+        ],
         compiler_params=params,
         name="strips",
-    )(*[near(v) for v in fields])
+    )(*[near(v) for v in fields + (region1,)])
     tokens, cot_fine, cot_coarse = fields
     small = (region1, region2, bias_index, bias_table1.T, bias_table2.T)
     kept = (
@@ -676,7 +750,7 @@
         partial(prepare_kernel, len(kept)),
         out_shape=[sds(*v.shape, dtype=v.dtype) for v in kept]
         + [
-            f32(n_tok, 128), f32(n_tok // 4, 128), f32(TOK, heads1 * TOK), f32(TOK, heads2 * TOK),
+            f32(n_tok // 2, 128), f32(n_tok // 8, 128), f32(heads1, TOK, 128), f32(heads2, TOK, 128),
             sds(TOK // 2, 2 * TOK, dtype=jnp.int32),
         ],
         in_specs=[pl.BlockSpec(memory_space=pltpu.VMEM)] + [far] * (len(small) + len(kept)),
@@ -687,27 +761,23 @@
         name="prepare",
     )(corner, *[near(v) for v in small + kept])
     row, col, corner = send(row, col, corner, -1)
-    xw, qkv, mixed, fs, fr, fc, fk = call(
+    xw, qkv, mixed, fs = call(
         fine_forward_kernel,
-        (
-            sds(n_tok, feat), sds(n_tok, 3 * feat), sds(n_tok, feat), sds(rc, cc, feat),
-            sds(nr, feat), sds(nc, feat), sds(nk, feat),
-        ),
-        [(rc + RIM, cc + 2 * RIM, feat), (rc, cc, feat)],
+        (sds(n_tok, feat), sds(n_tok, 3 * feat), sds(n_tok, feat), sds(rc, cc, feat)),
+        [(rc + EXTRA_ROWS, cc + EXTRA_COLS, feat), (rc + WIN, cc + WIN, feat)],
         tokens, row, col, corner, keys1, bias1, gain1, wqkv1, wout1,
     )
-    fr, fc, fk = send(fr, fc, fk, -1)
     cs, cfo, er, ec, ek, coarse_grads, gmgain, ggain2, gbias2 = call(
         coarse_kernel,
         (
             sds(2, r2, c2, feat), sds(rc, cc, feat), sds(nr, feat), sds(nc, feat), sds(nk, feat),
-            f32(2, COARSE, feat), f32(1, 4 * feat), f32(1, feat2), f32(TOK, heads2 * TOK),
+            f32(2, COARSE, feat), f32(1, 4 * feat), f32(1, feat2), f32(heads2, TOK, 2 * TOK),
         ),
         [
-            (rc + RIM, cc + 2 * RIM, feat), (rc + 2 * RIM, cc + 2 * RIM, feat),
+            (rc, cc, feat), (rc + 2 * RIM, cc + 2 * RIM, feat),
             (2, r2 + RIM, c2 + 2 * RIM, feat), (rc, cc, feat), (2, r2, c2, feat),
         ],
-        fs, fr, fc, fk, cot_fine, cot_coarse, row, col, corner,
+        fs, cot_fine, cot_coarse, row, col, corner,
         keys2, bias2, mgain, wmerge, gain2, wqkv2, wout2,
     )
     er, ec, ek = send(er, ec, ek, 1)

time: 113 us -> 107 us (0.947)
  starting transfers between devices: 40.3 us -> 34.7 us
  waiting for transfers between devices: 24.3 us -> 22.7 us
    ppermute x4 -> x3, starting transfers between devices: 10.6 us -> 6.44 us  [send(): lax.ppermute(corner, LON + LAT, both)]
    ppermute x4 -> x3, starting transfers between devices: 10.6 us -> 6.69 us  [send(): lax.ppermute(cols, LON, lon)]
    all_to_all x1, starting transfers between devices: 7.84 us -> 9.27 us  [along_torus(): return lax.all_to_all(values, CHIPS, 0, 0, tiled=False)]
    ppermute x4 -> x3, waiting for transfers between devices: 7.14 us -> 5.91 us  [send(): lax.ppermute(corner, LON + LAT, both)]
    ppermute x4 -> x3, starting transfers between devices: 4.72 us -> 4.87 us  [send(): lax.ppermute(rows, LAT, lat)]
  transfers between devices with their start and end apart: 15 -> 12, of which waited for: 5 -> 4; matrix products, arithmetic and copies ran while one was open for 0% -> 0% of each run, Pallas kernels for 3% -> 3%
where the time goes in v1:
time: 107 us
  starting transfers between devices  34.7 us (32%)
  blocking collectives  25.6 us (24%)
  Pallas kernels  23 us (21%)
  waiting for transfers between devices  22.7 us (21%)
    all_to_all x1, blocking collectives, along_torus(): return lax.all_to_all(values, CHIPS, 0, 0, tiled=False)  25.6 us
    pallas_call x7, Pallas kernels, call(): pl.pallas_call(kernel, name=getattr(kernel, 'func', kernel).__name__, out...  19.3 us
    all_to_all x1, waiting for transfers between devices, along_torus(): return lax.all_to_all(values, CHIPS, 0, 0, tiled=False)  13.8 us
    all_to_all x1, starting transfers between devices, along_torus(): return lax.all_to_all(values, CHIPS, 0, 0, tiled=False)  9.27 us
    ppermute x3, starting transfers between devices, send(): lax.ppermute(cols, LON, lon)  6.69 us
    ppermute x3, starting transfers between devices, send(): lax.ppermute(corner, LON + LAT, both)  6.44 us
    ppermute x3, waiting for transfers between devices, send(): lax.ppermute(corner, LON + LAT, both)  5.91 us
    ppermute x3, starting transfers between devices, send(): lax.ppermute(rows, LAT, lat)  4.87 us
  transfers between devices with their start and end apart: 12, of which 4 were waited for; matrix products, arithmetic and copies ran while one was open for 0% of the time, Pallas kernels for 3%

profile of v1, /device:TPU:1, one launch (start us, length us, event | category | flops | bytes accessed | tf_op | source)
XLA Modules:
  0.0 106.8 jit_solution(741681735199818984)
XLA Ops:
  0.6 1.2 %strips.1 = (bf16[16,64,128]{2,1,0:T(8,128)(2,1)S(1)}, bf16[16,64,128]{2,1,0:T(8,128)(2,1)S(1)}, bf16[8,32,256]{2,1,0:T(8,128)(2,1)S(1)}, bf16[1552,128]{1,0:T(8...) custom-call(bf16[16,64,128]{2,1,0:T(8,128)(2,1)} %x_in.1, bf16[16,64,128]{2,1,0:T(8,128)(2,1)} %cf_in.1, ...), custom_call_target="tpu_custom_call" | custom-call | tf_op jit(solution)/shard_map/strips/pallas_call | solution.py:730
  1.8 3.3 %collective-permute-start = (bf16[1552,128]{1,0:T(8,128)(2,1)S(1)}, bf16[1552,128]{1,0:T(8,128)(2,1)S(1)}, u32[]{:S(2)}, u32[]{:S(2)}) collective-permute-start(bf16[1552,128]{1,0:T(8,128)(2,1)S(1)} %get-tuple-element.67), channel_id=1, source_target_pairs={{0,15},{1,0},{2,1},{3,2},{4,3},{5,4},{6,5},{7,6},{8,7},{9,8},{10,9... | collective-permute-start | bytes 1191944 | tf_op jit(solution)/shard_map/ppermute | solution.py:704
  5.1 4.9 %collective-permute-start.1 = (bf16[464,128]{1,0:T(8,128)(2,1)S(1)}, bf16[464,128]{1,0:T(8,128)(2,1)S(1)}, u32[]{:S(2)}, u32[]{:S(2)}) collective-permute-start(bf16[464,128]{1,0:T(8,128)(2,1)S(1)} %get-tuple-element.68), channel_id=1, source_target_pairs={{0,240},{16,0},{32,16},{48,32},{64,48},{80,64},{96,80},{112,96},{1... | collective-permute-start | bytes 356360 | tf_op jit(solution)/shard_map/ppermute | solution.py:705
  10.0 5.2 %collective-permute-start.2 = (bf16[304,128]{1,0:T(8,128)(2,1)S(1)}, bf16[304,128]{1,0:T(8,128)(2,1)S(1)}, u32[]{:S(2)}, u32[]{:S(2)}) collective-permute-start(bf16[304,128]{1,0:T(8,128)(2,1)S(1)} %get-tuple-element.69.refs_0_), channel_id=1, source_target_pairs={{0,255},{16,15},{32,31},{48,47},{64,63},{80,79},{96,95},{112,111},... | collective-permute-start | bytes 233480 | tf_op jit(solution)/shard_map/ppermute | solution.py:706
  15.2 2.5 %prepare.1 = (f32[1,128]{1,0:T(1,128)S(1)}, f32[1,256]{1,0:T(1,128)S(1)}, f32[1,512]{1,0:T(1,128)S(1)}, bf16[128,384]{1,0:T(8,128)(2,1)S(1)}, bf16[128,128]{1,0:...) custom-call(bf16[304,128]{1,0:T(8,128)(2,1)S(1)} %get-tuple-element., ...), custom_call_target="tpu_custom_call" | custom-call | tf_op jit(solution)/shard_map/prepare/pallas_call | solution.py:749
  17.6 0.0 collective-permute-done.2.xk.ck
  17.6 0.0 collective-permute-done.1.xc.ccl
  17.7 0.0 collective-permute-done.xr.cr
  17.7 5.6 %fine_forward_kernel.1 = (bf16[1024,128]{1,0:T(8,128)(2,1)S(1)}, bf16[1024,384]{1,0:T(8,128)(2,1)S(1)}, bf16[1024,128]{1,0:T(8,128)(2,1)S(1)}, bf16[16,64,128]{2,1,0:T(8,128)(2,1)S(1)}) custom-call(bf16[16,64,128]{2,1,0:T(8,128)(2,1)S(1)} %get-tuple-element.66.x, bf16[1552,128]{1,0:T(8,128)(2,1)S(1)} %collective-permute-done.xr.cr, ...), custom_call_target="tpu_custom_call" | custom-call | tf_op jit(solution)/shard_map/fine_forward_kernel/pallas_call | solution.py:681
  23.3 4.2 %coarse_kernel.1 = (bf16[2,8,32,128]{3,2,1,0:T(8,128)(2,1)S(1)}, bf16[16,64,128]{2,1,0:T(8,128)(2,1)S(1)}, bf16[256,128]{1,0:T(8,128)(2,1)S(1)}, bf16[64,128]{1,...) custom-call(bf16[16,64,128]{2,1,0:T(8,128)(2,1)S(1)} %get-tuple-elem, ...), custom_call_target="tpu_custom_call" | custom-call | tf_op jit(solution)/shard_map/coarse_kernel/pallas_call | solution.py:681
  27.6 0.1 collective-permute-start.3
  27.6 0.7 collective-permute-start.4
  28.3 0.0 collective-permute-start.5
  28.3 5.9 %collective-permute-done.5.ek = bf16[16,128]{1,0:T(8,128)(2,1)S(1)} collective-permute-done((bf16[16,128]{1,0:T(8,128)(2,1)S(1)}, bf16[16,128]{1,0:T(8,128)(2,1)S(1)}, u32[]{:S(2)}, u32[]{:S(2)}) %collective-permute-start.5) | collective-permute-done | bytes 4128 | tf_op jit(solution)/shard_map/ppermute | solution.py:706
  34.2 0.0 collective-permute-done.4.ec
  34.2 0.0 collective-permute-done.3.er
  34.2 6.2 %fine_backward_kernel.1 = (bf16[16,64,128]{2,1,0:T(8,128)(2,1)S(1)}, bf16[512,128]{1,0:T(8,128)(2,1)S(1)}, bf16[128,128]{1,0:T(8,128)(2,1)S(1)}, bf16[48,128]{1,...) custom-call(bf16[16,64,128]{2,1,0:T(8,128)(2,1)S(1)} %get-tuple-element.85.c, ...), custom_call_target="tpu_custom_call" | custom-call | tf_op jit(solution)/shard_map/fine_backward_kernel/pallas_call | solution.py:681
  40.4 4.4 %collective-permute-start.6 = (f32[2048,128]{1,0:T(8,128)S(1)}, f32[2048,128]{1,0:T(8,128)S(1)}, u32[]{:S(2)}, u32[]{:S(2)}) collective-permute-start(f32[2048,128]{1,0:T(8,128)S(1)} %get-tuple-element.100), channel_id=1, source_target_pairs={{0,1},{1,0},{2,3},{3,2},{4,5},{5,4},{6,7},{7,6},{8,9},{9,8},{10,11... | collective-permute-start | bytes 3145736 | tf_op jit(solution)/shard_map/ppermute | solution.py:797
  44.7 2.3 %collective-permute-done.6.got = f32[2048,128]{1,0:T(8,128)S(1)} collective-permute-done((f32[2048,128]{1,0:T(8,128)S(1)}, f32[2048,128]{1,0:T(8,128)S(1)}, u32[]{:S(2)}, u32[]{:S(2)}) %collective-permute-start.6) | collective-permute-done | bytes 1048608 | tf_op jit(solution)/shard_map/ppermute | solution.py:797
  47.0 1.0 cores_kernel.1
  48.0 9.3 %all-to-all-start = ((bf16[128,16,128]{2,1,0:T(8,128)(2,1)}), bf16[128,16,128]{2,1,0:T(8,128)(2,1)S(1)}, u32[]{:S(2)}, u32[]{:S(2)}) async-start(bf16[128,16,128]{2,1,0:T(8,128)(2,1)} %cores_kernel.1), calls=%async_computation | async-start | bytes 1048576 | tf_op jit(solution)/shard_map/all_to_all | solution.py:711
  57.3 1.5 %collective-permute-start.7 = (bf16[512,128]{1,0:T(8,128)(2,1)S(1)}, bf16[512,128]{1,0:T(8,128)(2,1)S(1)}, u32[]{:S(2)}, u32[]{:S(2)}) collective-permute-start(bf16[512,128]{1,0:T(8,128)(2,1)S(1)} %get-tuple-element.101), channel_id=1, source_target_pairs={{0,1},{1,2},{2,3},{3,4},{4,5},{5,6},{6,7},{7,8},{8,9},{9,10},{10,1... | collective-permute-start | bytes 393224 | tf_op jit(solution)/shard_map/ppermute | solution.py:704
  58.7 1.2 %collective-permute-start.8 = (bf16[128,128]{1,0:T(8,128)(2,1)S(1)}, bf16[128,128]{1,0:T(8,128)(2,1)S(1)}, u32[]{:S(2)}, u32[]{:S(2)}) collective-permute-start(bf16[128,128]{1,0:T(8,128)(2,1)S(1)} %get-tuple-element.102), channel_id=1, source_target_pairs={{0,16},{16,32},{32,48},{48,64},{64,80},{80,96},{96,112},{112,128},... | collective-permute-start | bytes 98312 | tf_op jit(solution)/shard_map/ppermute | solution.py:705
  59.9 1.3 %collective-permute-start.9 = (bf16[48,128]{1,0:T(8,128)(2,1)S(1)}, bf16[48,128]{1,0:T(8,128)(2,1)S(1)}, u32[]{:S(2)}, u32[]{:S(2)}) collective-permute-start(bf16[48,128]{1,0:T(8,128)(2,1)S(1)} %get-tuple-element.103), channel_id=1, source_target_pairs={{0,17},{16,33},{32,49},{48,65},{64,81},{80,97},{96,113},{112,129},... | collective-permute-start | bytes 36872 | tf_op jit(solution)/shard_map/ppermute | solution.py:706
  61.2 13.8 %all-to-all-done.parts = bf16[128,16,128]{2,1,0:T(8,128)(2,1)S(1)} async-done(((bf16[128,16,128]{2,1,0:T(8,128)(2,1)}), bf16[128,16,128]{2,1,0:T(8,128)(2,1)S(1)}, u32[]{:S(2)}, u32[]{:S(2)}) %all-to-all-start) | async-done | bytes 524320 | tf_op jit(solution)/shard_map/all_to_all | solution.py:711
  75.0 0.2 sum_kernel.1
  75.1 0.0 collective-permute-done.9.ek
  75.1 0.0 collective-permute-done.8.ec
  75.2 0.0 collective-permute-done.7.er
  75.2 25.6 %all_to_all.10.own = bf16[128,16,128]{2,1,0:T(8,128)(2,1)S(1)} all-to-all(bf16[128,16,128]{2,1,0:T(8,128)(2,1)S(1)} %sum_kernel.1), channel_id=1, replica_groups=mesh['z'=8,'yl'=2,'yh'=2,'x'=4,'c'=2] {'z','yl','yh','x'}, dimensions={0} | all-to-all | bytes 1048576 | tf_op jit(solution)/shard_map/all_to_all | solution.py:711
  100.8 3.1 %collective-permute-start.10 = (bf16[128,16,128]{2,1,0:T(8,128)(2,1)S(1)}, bf16[128,16,128]{2,1,0:T(8,128)(2,1)S(1)}, u32[]{:S(2)}, u32[]{:S(2)}) collective-permute-start(bf16[128,16,128]{2,1,0:T(8,128)(2,1)S(1)} %all_to_all.10.own), channel_id=1, source_target_pairs={{0,1},{1,0},{2,3},{3,2},{4,5},{5,4},{6,7},{7,6},{8,9},{9,8},{10,11... | collective-permute-start | bytes 1572872 | tf_op jit(solution)/shard_map/ppermute | solution.py:819
  103.9 0.8 place_kernel.1
  104.7 0.7 collective-permute-done.10.got
  105.4 1.3 %unpack_kernel.1 = (f32[1,128]{1,0:T(1,128)}, f32[128,384]{1,0:T(8,128)}, f32[128,128]{1,0:T(8,128)}, f32[4,225]{1,0:T(4,128)}, f32[1,512]{1,0:T(1,128)}, /*inde...) custom-call(bf16[128,16,128]{2,1,0:T(8,128)(2,1)S(1)} %all_to_all.10.own, ...), custom_call_target="tpu_custom_call" | custom-call | tf_op jit(solution)/shard_map/unpack_kernel/pallas_call | solution.py:681
Async XLA Ops:
  1.8 15.8 %collective-permute-start = (bf16[1552,128]{1,0:T(8,128)(2,1)S(1)}, bf16[1552,128]{1,0:T(8,128)(2,1)S(1)}, u32[]{:S(2)}, u32[]{:S(2)}) collective-permute-start(bf16[1552,128]{1,0:T(8,128)(2,1)S(1)} %get-tuple-element.67), channel_id=1, source_target_pairs={{0,15},{1,0},{2,1},{3,2},{4,3},{5,4},{6,5},{7,6},{8,7},{9,8},{10,9... | collective-permute-start | bytes 1191944 | tf_op jit(solution)/shard_map/ppermute | solution.py:704
  5.1 12.5 %collective-permute-start.1 = (bf16[464,128]{1,0:T(8,128)(2,1)S(1)}, bf16[464,128]{1,0:T(8,128)(2,1)S(1)}, u32[]{:S(2)}, u32[]{:S(2)}) collective-permute-start(bf16[464,128]{1,0:T(8,128)(2,1)S(1)} %get-tuple-element.68), channel_id=1, source_target_pairs={{0,240},{16,0},{32,16},{48,32},{64,48},{80,64},{96,80},{112,96},{1... | collective-permute-start | bytes 356360 | tf_op jit(solution)/shard_map/ppermute | solution.py:705
  10.0 7.6 %collective-permute-start.2 = (bf16[304,128]{1,0:T(8,128)(2,1)S(1)}, bf16[304,128]{1,0:T(8,128)(2,1)S(1)}, u32[]{:S(2)}, u32[]{:S(2)}) collective-permute-start(bf16[304,128]{1,0:T(8,128)(2,1)S(1)} %get-tuple-element.69.refs_0_), channel_id=1, source_target_pairs={{0,255},{16,15},{32,31},{48,47},{64,63},{80,79},{96,95},{112,111},... | collective-permute-start | bytes 233480 | tf_op jit(solution)/shard_map/ppermute | solution.py:706
  27.6 6.7 %collective-permute-start.3 = (bf16[256,128]{1,0:T(8,128)(2,1)S(1)}, bf16[256,128]{1,0:T(8,128)(2,1)S(1)}, u32[]{:S(2)}, u32[]{:S(2)}) collective-permute-start(bf16[256,128]{1,0:T(8,128)(2,1)S(1)} %get-tuple-element.87), channel_id=1, source_target_pairs={{0,1},{1,2},{2,3},{3,4},{4,5},{5,6},{6,7},{7,8},{8,9},{9,10},{10,1... | collective-permute-start | bytes 196616 | tf_op jit(solution)/shard_map/ppermute | solution.py:704
  27.6 6.6 %collective-permute-start.4 = (bf16[64,128]{1,0:T(8,128)(2,1)S(1)}, bf16[64,128]{1,0:T(8,128)(2,1)S(1)}, u32[]{:S(2)}, u32[]{:S(2)}) collective-permute-start(bf16[64,128]{1,0:T(8,128)(2,1)S(1)} %get-tuple-element.88), channel_id=1, source_target_pairs={{0,16},{16,32},{32,48},{48,64},{64,80},{80,96},{96,112},{112,128},... | collective-permute-start | bytes 49160 | tf_op jit(solution)/shard_map/ppermute | solution.py:705
  28.3 5.9 %collective-permute-start.5 = (bf16[16,128]{1,0:T(8,128)(2,1)S(1)}, bf16[16,128]{1,0:T(8,128)(2,1)S(1)}, u32[]{:S(2)}, u32[]{:S(2)}) collective-permute-start(bf16[16,128]{1,0:T(8,128)(2,1)S(1)} %get-tuple-element.89), channel_id=1, source_target_pairs={{0,17},{16,33},{32,49},{48,65},{64,81},{80,97},{96,113},{112,129},... | collective-permute-start | bytes 12296 | tf_op jit(solution)/shard_map/ppermute | solution.py:706
  40.4 6.6 %collective-permute-start.6 = (f32[2048,128]{1,0:T(8,128)S(1)}, f32[2048,128]{1,0:T(8,128)S(1)}, u32[]{:S(2)}, u32[]{:S(2)}) collective-permute-start(f32[2048,128]{1,0:T(8,128)S(1)} %get-tuple-element.100), channel_id=1, source_target_pairs={{0,1},{1,0},{2,3},{3,2},{4,5},{5,4},{6,7},{7,6},{8,9},{9,8},{10,11... | collective-permute-start | bytes 3145736 | tf_op jit(solution)/shard_map/ppermute | solution.py:797
  48.0 27.0 %all-to-all-start = ((bf16[128,16,128]{2,1,0:T(8,128)(2,1)}), bf16[128,16,128]{2,1,0:T(8,128)(2,1)S(1)}, u32[]{:S(2)}, u32[]{:S(2)}) async-start(bf16[128,16,128]{2,1,0:T(8,128)(2,1)} %cores_kernel.1), calls=%async_computation | async-start | bytes 1048576 | tf_op jit(solution)/shard_map/all_to_all | solution.py:711
  57.3 17.9 %collective-permute-start.7 = (bf16[512,128]{1,0:T(8,128)(2,1)S(1)}, bf16[512,128]{1,0:T(8,128)(2,1)S(1)}, u32[]{:S(2)}, u32[]{:S(2)}) collective-permute-start(bf16[512,128]{1,0:T(8,128)(2,1)S(1)} %get-tuple-element.101), channel_id=1, source_target_pairs={{0,1},{1,2},{2,3},{3,4},{4,5},{5,6},{6,7},{7,8},{8,9},{9,10},{10,1... | collective-permute-start | bytes 393224 | tf_op jit(solution)/shard_map/ppermute | solution.py:704
  58.7 16.4 %collective-permute-start.8 = (bf16[128,128]{1,0:T(8,128)(2,1)S(1)}, bf16[128,128]{1,0:T(8,128)(2,1)S(1)}, u32[]{:S(2)}, u32[]{:S(2)}) collective-permute-start(bf16[128,128]{1,0:T(8,128)(2,1)S(1)} %get-tuple-element.102), channel_id=1, source_target_pairs={{0,16},{16,32},{32,48},{48,64},{64,80},{80,96},{96,112},{112,128},... | collective-permute-start | bytes 98312 | tf_op jit(solution)/shard_map/ppermute | solution.py:705
  59.9 15.2 %collective-permute-start.9 = (bf16[48,128]{1,0:T(8,128)(2,1)S(1)}, bf16[48,128]{1,0:T(8,128)(2,1)S(1)}, u32[]{:S(2)}, u32[]{:S(2)}) collective-permute-start(bf16[48,128]{1,0:T(8,128)(2,1)S(1)} %get-tuple-element.103), channel_id=1, source_target_pairs={{0,17},{16,33},{32,49},{48,65},{64,81},{80,97},{96,113},{112,129},... | collective-permute-start | bytes 36872 | tf_op jit(solution)/shard_map/ppermute | solution.py:706
  100.8 4.6 %collective-permute-start.10 = (bf16[128,16,128]{2,1,0:T(8,128)(2,1)S(1)}, bf16[128,16,128]{2,1,0:T(8,128)(2,1)S(1)}, u32[]{:S(2)}, u32[]{:S(2)}) collective-permute-start(bf16[128,16,128]{2,1,0:T(8,128)(2,1)S(1)} %all_to_all.10.own), channel_id=1, source_target_pairs={{0,1},{1,0},{2,3},{3,2},{4,5},{5,4},{6,7},{7,6},{8,9},{9,8},{10,11... | collective-permute-start | bytes 1572872 | tf_op jit(solution)/shard_map/ppermute | solution.py:819

commit v2 on v1

--- a/solution.py
+++ b/solution.py
@@ -64,15 +64,19 @@
     )
 
 
-def by_query(weights, pair):
-    turned = jnp.concatenate([weights[h] for h in range(4)], 1).T
-    out = []
-    for w in range(2):
-        rows = jnp.concatenate(
-            [turned[(2 * h + w) * TOK : (2 * h + w + 1) * TOK] for h in range(4)], 0
-        )
-        out.append(fold_heads(nn_dot(rows, pair[w])).astype(BF16))
-    return out
+def by_query(weights, pairs):
+    turned = [jnp.concatenate([p[h] for h in range(4)], 1).T for p in weights]
+    rows = [
+        [
+            jnp.concatenate(
+                [t[(2 * h + w) * TOK : (2 * h + w + 1) * TOK] for h in range(4)], 0
+            )
+            for w in range(2)
+        ]
+        for t in turned
+    ]
+    wide = [[nn_dot(r[w], pair[w]) for w in range(2)] for r, pair in zip(rows, pairs)]
+    return [[fold_heads(w).astype(BF16) for w in both] for both in wide]
 
 
 def by_key(weights, spread):
@@ -81,25 +85,36 @@
 
 
 def probs(k4, q2, bias, same):
-    scores = nt_dot(k4, q2).reshape(4, TOK, 2 * TOK) * (32 ** (-0.5)) + bias
-    scores = jnp.where(same[None] > 0.5, scores, MASKED)
-    top = jnp.max(scores, axis=1, keepdims=True)
-    grown = jnp.exp(scores - top)
-    return grown * (1.0 / jnp.sum(grown, axis=1, keepdims=True))
-
-
-def unit_forward(q, k, v, bias, same, hm):
-    weights = probs(spread_heads(k, hm), diagonal(q), bias, same).astype(BF16)
-    return by_query(weights, v)
-
-
-def unit_backward(q, k, v, g, bias, same, hm):
-    q2, g2 = diagonal(q), diagonal(g)
-    p = probs(spread_heads(k, hm), q2, bias, same)
-    dp = nt_dot(spread_heads(v, hm), g2).astype(BF16).astype(F32).reshape(p.shape)
-    ds = p * (dp - jnp.sum(p * dp, axis=1, keepdims=True))
-    dsb = (ds * (32 ** (-0.5))).astype(BF16)
-    return by_query(dsb, k), by_key(dsb, q2), by_key(p.astype(BF16), g2), ds
+    scores = [nt_dot(k, q).reshape(4, TOK, 2 * TOK) for k, q in zip(k4, q2)]
+    scores = [
+        jnp.where(m[None] > 0.5, s * (32 ** (-0.5)) + b, MASKED)
+        for s, b, m in zip(scores, bias, same)
+    ]
+    tops = [jnp.max(s, axis=1, keepdims=True) for s in scores]
+    grown = [jnp.exp(s - top) for s, top in zip(scores, tops)]
+    sums = [jnp.sum(e, axis=1, keepdims=True) for e in grown]
+    return [e * (1.0 / total) for e, total in zip(grown, sums)]
+
+
+def units_forward(units, hm):
+    q, k, v, bias, same = zip(*units)
+    ps = probs([spread_heads(p, hm) for p in k], [diagonal(p) for p in q], bias, same)
+    return by_query([p.astype(BF16) for p in ps], v)
+
+
+def units_backward(units, hm):
+    q, k, v, g, bias, same = zip(*units)
+    q2 = [diagonal(p) for p in q]
+    g2 = [diagonal(p) for p in g]
+    ps = probs([spread_heads(p, hm) for p in k], q2, bias, same)
+    dps = [nt_dot(spread_heads(p, hm), d) for p, d in zip(v, g2)]
+    dps = [dp.astype(BF16).astype(F32).reshape(p.shape) for dp, p in zip(dps, ps)]
+    sums = [jnp.sum(p * dp, axis=1, keepdims=True) for p, dp in zip(ps, dps)]
+    dss = [p * (dp - total) for p, dp, total in zip(ps, dps, sums)]
+    dsb = [(ds * (32 ** (-0.5))).astype(BF16) for ds in dss]
+    dks = [by_key(d, p) for d, p in zip(dsb, q2)]
+    dvs = [by_key(p.astype(BF16), d) for p, d in zip(ps, g2)]
+    return list(zip(by_query(dsb, k), dks, dvs, dss))
 
 
 def same_keys(first, second):
@@ -342,45 +357,41 @@
     own = [(a, b) for a in range(rows) for b in range(cols)]
     more = [(a, cols) for a in range(rows)] + [(rows, b) for b in range(cols + 1)]
     more = more + more[-1:] * (len(more) % 2)
-    group = 4
-    for windows in (own, more):
-        for n0 in range(0, len(windows), group):
-            now = windows[n0 : n0 + group]
-            tokens = jnp.concatenate(
-                [
-                    field[
-                        RIM + WIN * a : RIM + WIN * (a + 1), RIM + WIN * b : RIM + WIN * (b + 1), :
-                    ].reshape(TOK, feat)
-                    for a, b in now
-                ],
-                0,
-            )
-            hat, _ = unit_norm(tokens)
-            normed = (hat * gain[...]).astype(BF16)
-            qkv = nn_dot(normed, wqkv[...]).astype(BF16)
-            mixed = []
-            for n in range(0, len(now), 2):
-                parts = [
-                    [qkv[m * TOK : (m + 1) * TOK, i * feat : (i + 1) * feat] for m in (n, n + 1)]
-                    for i in range(3)
-                ]
-                if windows is own:
-                    pair = (n0 + n) // 2
-                    same = keys[pair * TOK : (pair + 1) * TOK, :]
-                else:
-                    same = same_keys(onehot(*now[n]), onehot(*now[n + 1]))
-                mixed += unit_forward(*parts, bias[...], same, hm)
-            mixed = jnp.concatenate(mixed, 0)
-            if windows is own:
-                span = pl.ds(n0 * TOK, group * TOK)
-                xw_out[span, :] = tokens.astype(BF16)
-                qkv_out[span, :] = qkv
-                mixed_out[span, :] = mixed
-            result = tokens + nn_dot(mixed, wout[...])
-            for n, (a, b) in enumerate(now):
-                grid[WIN * a : WIN * (a + 1), WIN * b : WIN * (b + 1), :] = result[
-                    n * TOK : (n + 1) * TOK
-                ].reshape(WIN, WIN, feat)
+    now = own + more
+    tokens = jnp.concatenate(
+        [
+            field[
+                RIM + WIN * a : RIM + WIN * (a + 1), RIM + WIN * b : RIM + WIN * (b + 1), :
+            ].reshape(TOK, feat)
+            for a, b in now
+        ],
+        0,
+    )
+    hat, _ = unit_norm(tokens)
+    normed = (hat * gain[...]).astype(BF16)
+    qkv = nn_dot(normed, wqkv[...]).astype(BF16)
+    units = []
+    for n in range(0, len(now), 2):
+        parts = [
+            [qkv[m * TOK : (m + 1) * TOK, i * feat : (i + 1) * feat] for m in (n, n + 1)]
+            for i in range(3)
+        ]
+        if n < len(own):
+            same = keys[n // 2 * TOK : (n // 2 + 1) * TOK, :]
+        else:
+            same = same_keys(onehot(*now[n]), onehot(*now[n + 1]))
+        units.append((*parts, bias[...], same))
+    mixed = sum(units_forward(units, hm), [])
+    mixed = jnp.concatenate(mixed, 0)
+    count = len(own) * TOK
+    xw_out[...] = tokens[:count].astype(BF16)
+    qkv_out[...] = qkv[:count]
+    mixed_out[...] = mixed[:count]
+    result = tokens + nn_dot(mixed, wout[...])
+    for n, (a, b) in enumerate(now):
+        grid[WIN * a : WIN * (a + 1), WIN * b : WIN * (b + 1), :] = result[
+            n * TOK : (n + 1) * TOK
+        ].reshape(WIN, WIN, feat)
     out[...] = grid[RIM : RIM + rc, RIM : RIM + cc, :].astype(BF16)
 
 
@@ -460,16 +471,21 @@
         lo = i * feat2 + g * feat
         return [wide[m * TOK : (m + 1) * TOK, lo : lo + feat] for m in (w, w + 1)]
 
-    mixed = []
-    for w in range(0, len(windows), 2):
-        same = keys[w // 2 * TOK : (w // 2 + 1) * TOK, :]
-        units = [
-            unit_forward(
-                *[parts_of(qkv, w, i, g) for i in range(3)], bias[4 * g : 4 * g + 4], same, hm
-            )
-            for g in range(2)
-        ]
-        mixed += [jnp.concatenate([units[0][m], units[1][m]], 1) for m in range(2)]
+    pairs = [(w, g) for w in range(0, len(windows), 2) for g in range(2)]
+    units = [
+        (
+            *[parts_of(qkv, w, i, g) for i in range(3)],
+            bias[4 * g : 4 * g + 4],
+            keys[w // 2 * TOK : (w // 2 + 1) * TOK, :],
+        )
+        for w, g in pairs
+    ]
+    found = dict(zip(pairs, units_forward(units, hm)))
+    mixed = [
+        jnp.concatenate([found[w, 0][m], found[w, 1][m]], 1)
+        for w in range(0, len(windows), 2)
+        for m in range(2)
+    ]
     mixed = jnp.concatenate(mixed, 0)
     result = coarse_in + nn_dot(mixed, wout[...])
     for w, (a, b) in enumerate(windows):
@@ -497,23 +513,15 @@
         packed[1, b * feat2 : (b + 1) * feat2, :] = grad[:, b * feat : (b + 1) * feat]
     cot_mixed = nt_dot(cotb, wout[...]).astype(BF16)
     cot_rows = []
-    total = [0.0, 0.0]
+    units = [
+        (*unit[:3], parts_of(cot_mixed, w, 0, g), *unit[3:]) for (w, g), unit in zip(pairs, units)
+    ]
+    found = dict(zip(pairs, units_backward(units, hm)))
+    total = [sum(found[w, g][3] for w in range(0, len(windows), 2)) for g in range(2)]
     for w in range(0, len(windows), 2):
-        same = keys[w // 2 * TOK : (w // 2 + 1) * TOK, :]
-        found = []
-        for g in range(2):
-            dq, dk, dv, ds = unit_backward(
-                *[parts_of(qkv, w, i, g) for i in range(3)],
-                parts_of(cot_mixed, w, 0, g),
-                bias[4 * g : 4 * g + 4],
-                same,
-                hm,
-            )
-            found.append((dq, dk, dv))
-            total[g] = total[g] + ds
         for m in range(2):
             cot_rows.append(
-                jnp.concatenate([found[g][i][m] for i in range(3) for g in range(2)], 1)
+                jnp.concatenate([found[w, g][i][m] for i in range(3) for g in range(2)], 1)
             )
     for g in range(2):
         gbias[4 * g : 4 * g + 4] = total[g]
@@ -567,56 +575,53 @@
     pushed(field, c[...], er[...], ec[...], ek[...], RIM, rc, cc)
     hm = head_masks()
     wide = cc // WIN
-    group = 4
+    group = 16
     total = jnp.zeros((4, TOK, 2 * TOK), F32)
     total_gain = jnp.zeros((1, feat), F32)
     total_out = jnp.zeros((feat, feat), F32)
     total_qkv = jnp.zeros((feat, 3 * feat), F32)
-    for a in range(rc // WIN):
-        for b0 in range(0, wide, group):
-            cot = jnp.concatenate(
-                [
-                    field[
-                        WIN * a : WIN * (a + 1), WIN * b : WIN * (b + 1), :
-                    ].reshape(TOK, feat)
-                    for b in range(b0, b0 + group)
-                ],
-                0,
-            )
-            t0 = (a * wide + b0) * TOK
-            span = pl.ds(t0, group * TOK)
-            cotb = cot.astype(BF16)
-            total_out = total_out + tn_dot(mixed_in[span, :], cotb)
-            cot_mixed = nt_dot(cotb, wout[...]).astype(BF16)
-            qkv = qkv_in[span, :]
-            cot_rows = []
-            for n in range(0, group, 2):
-                pair = (a * wide + b0 + n) // 2
-                parts = [
-                    [qkv[m * TOK : (m + 1) * TOK, i * feat : (i + 1) * feat] for m in (n, n + 1)]
-                    for i in range(3)
-                ]
-                dq, dk, dv, ds = unit_backward(
-                    *parts,
-                    [cot_mixed[m * TOK : (m + 1) * TOK] for m in (n, n + 1)],
-                    bias[...],
-                    keys[pair * TOK : (pair + 1) * TOK, :],
-                    hm,
-                )
-                total = total + ds
-                cot_rows += [jnp.concatenate([dq[m], dk[m], dv[m]], 1) for m in range(2)]
-            cot_qkv = jnp.concatenate(cot_rows, 0)
-            hat, rstd = unit_norm(xw[span, :].astype(F32))
-            normed = (hat * gain[...]).astype(BF16)
-            total_qkv = total_qkv + tn_dot(normed, cot_qkv)
-            cot_unit = nt_dot(cot_qkv, wqkv[...]).astype(BF16).astype(F32)
-            total_gain = total_gain + jnp.sum(cot_unit * hat, axis=0, keepdims=True)
-            result = cot + norm_back(hat, rstd, cot_unit, gain[...])
-            for n in range(group):
-                b = b0 + n
-                grid[WIN * a : WIN * (a + 1), WIN * b : WIN * (b + 1), :] = result[
-                    n * TOK : (n + 1) * TOK
-                ].reshape(WIN, WIN, feat)
+    windows = [(a, b) for a in range(rc // WIN) for b in range(wide)]
+    for n0 in range(0, len(windows), group):
+        now = windows[n0 : n0 + group]
+        cot = jnp.concatenate(
+            [
+                field[
+                    WIN * a : WIN * (a + 1), WIN * b : WIN * (b + 1), :
+                ].reshape(TOK, feat)
+                for a, b in now
+            ],
+            0,
+        )
+        t0 = n0 * TOK
+        span = pl.ds(t0, group * TOK)
+        cotb = cot.astype(BF16)
+        total_out = total_out + tn_dot(mixed_in[span, :], cotb)
+        cot_mixed = nt_dot(cotb, wout[...]).astype(BF16)
+        qkv = qkv_in[span, :]
+        cot_rows = []
+        units = []
+        for n in range(0, group, 2):
+            pair = (n0 + n) // 2
+            parts = [
+                [qkv[m * TOK : (m + 1) * TOK, i * feat : (i + 1) * feat] for m in (n, n + 1)]
+                for i in range(3)
+            ]
+            parts.append([cot_mixed[m * TOK : (m + 1) * TOK] for m in (n, n + 1)])
+            units.append((*parts, bias[...], keys[pair * TOK : (pair + 1) * TOK, :]))
+        for dq, dk, dv, ds in units_backward(units, hm):
+            total = total + ds
+            cot_rows += [jnp.concatenate([dq[m], dk[m], dv[m]], 1) for m in range(2)]
+        cot_qkv = jnp.concatenate(cot_rows, 0)
+        hat, rstd = unit_norm(xw[span, :].astype(F32))
+        normed = (hat * gain[...]).astype(BF16)
+        total_qkv = total_qkv + tn_dot(normed, cot_qkv)
+        cot_unit = nt_dot(cot_qkv, wqkv[...]).astype(BF16).astype(F32)
+        total_gain = total_gain + jnp.sum(cot_unit * hat, axis=0, keepdims=True)
+        result = cot + norm_back(hat, rstd, cot_unit, gain[...])
+        for n, (a, b) in enumerate(now):
+            grid[WIN * a : WIN * (a + 1), WIN * b : WIN * (b + 1), :] = result[
+                n * TOK : (n + 1) * TOK
+            ].reshape(WIN, WIN, feat)
     for b in range(3):
         packed[0, b * feat : (b + 1) * feat, :] = total_qkv[:, b * feat : (b + 1) * feat]
     packed[0, 3 * feat :, :] = jnp.zeros((feat, feat), F32)

time: 107 us -> 100 us (0.935)
  Pallas kernels: 23 us -> 16.4 us
    pallas_call x7, Pallas kernels: 19.3 us -> 12.7 us  [call(): pl.pallas_call(kernel, name=getattr(kernel, 'func', kernel).__name__, out...]
where the time goes in v2:
time: 100 us
  starting transfers between devices  34.5 us (34%)
  blocking collectives  25.7 us (26%)
  waiting for transfers between devices  22.8 us (23%)
  Pallas kernels  16.4 us (16%)
    all_to_all x1, blocking collectives, along_torus(): return lax.all_to_all(values, CHIPS, 0, 0, tiled=False)  25.7 us
    all_to_all x1, waiting for transfers between devices, along_torus(): return lax.all_to_all(values, CHIPS, 0, 0, tiled=False)  13.8 us
    pallas_call x7, Pallas kernels, call(): pl.pallas_call(kernel, name=getattr(kernel, 'func', kernel).__name__, out...  12.7 us
    all_to_all x1, starting transfers between devices, along_torus(): return lax.all_to_all(values, CHIPS, 0, 0, tiled=False)  9.26 us
    ppermute x3, starting transfers between devices, send(): lax.ppermute(cols, LON, lon)  6.52 us
    ppermute x3, starting transfers between devices, send(): lax.ppermute(corner, LON + LAT, both)  6.44 us
    ppermute x3, waiting for transfers between devices, send(): lax.ppermute(corner, LON + LAT, both)  6 us
    ppermute x3, starting transfers between devices, send(): lax.ppermute(rows, LAT, lat)  4.76 us
  transfers between devices with their start and end apart: 12, of which 4 were waited for; matrix products, arithmetic and copies ran while one was open for 0% of the time, Pallas kernels for 3%

profile of v2, /device:TPU:1, one launch (start us, length us, event | category | flops | bytes accessed | tf_op | source)
XLA Modules:
  0.0 100.2 jit_solution(11864697157533877940)
XLA Ops:
  0.6 1.2 %strips.1 = (bf16[16,64,128]{2,1,0:T(8,128)(2,1)S(1)}, bf16[16,64,128]{2,1,0:T(8,128)(2,1)S(1)}, bf16[8,32,256]{2,1,0:T(8,128)(2,1)S(1)}, bf16[1552,128]{1,0:T(8...) custom-call(bf16[16,64,128]{2,1,0:T(8,128)(2,1)} %x_in.1, bf16[16,64,128]{2,1,0:T(8,128)(2,1)} %cf_in.1, ...), custom_call_target="tpu_custom_call" | custom-call | tf_op jit(solution)/shard_map/strips/pallas_call | solution.py:735
  1.8 3.3 %collective-permute-start = (bf16[1552,128]{1,0:T(8,128)(2,1)S(1)}, bf16[1552,128]{1,0:T(8,128)(2,1)S(1)}, u32[]{:S(2)}, u32[]{:S(2)}) collective-permute-start(bf16[1552,128]{1,0:T(8,128)(2,1)S(1)} %get-tuple-element.67), channel_id=1, source_target_pairs={{0,15},{1,0},{2,1},{3,2},{4,3},{5,4},{6,5},{7,6},{8,7},{9,8},{10,9... | collective-permute-start | bytes 1191944 | tf_op jit(solution)/shard_map/ppermute | solution.py:709
  5.1 4.9 %collective-permute-start.1 = (bf16[464,128]{1,0:T(8,128)(2,1)S(1)}, bf16[464,128]{1,0:T(8,128)(2,1)S(1)}, u32[]{:S(2)}, u32[]{:S(2)}) collective-permute-start(bf16[464,128]{1,0:T(8,128)(2,1)S(1)} %get-tuple-element.68), channel_id=1, source_target_pairs={{0,240},{16,0},{32,16},{48,32},{64,48},{80,64},{96,80},{112,96},{1... | collective-permute-start | bytes 356360 | tf_op jit(solution)/shard_map/ppermute | solution.py:710
  10.0 5.2 %collective-permute-start.2 = (bf16[304,128]{1,0:T(8,128)(2,1)S(1)}, bf16[304,128]{1,0:T(8,128)(2,1)S(1)}, u32[]{:S(2)}, u32[]{:S(2)}) collective-permute-start(bf16[304,128]{1,0:T(8,128)(2,1)S(1)} %get-tuple-element.69.refs_0_), channel_id=1, source_target_pairs={{0,255},{16,15},{32,31},{48,47},{64,63},{80,79},{96,95},{112,111},... | collective-permute-start | bytes 233480 | tf_op jit(solution)/shard_map/ppermute | solution.py:711
  15.2 2.5 %prepare.1 = (f32[1,128]{1,0:T(1,128)S(1)}, f32[1,256]{1,0:T(1,128)S(1)}, f32[1,512]{1,0:T(1,128)S(1)}, bf16[128,384]{1,0:T(8,128)(2,1)S(1)}, bf16[128,128]{1,0:...) custom-call(bf16[304,128]{1,0:T(8,128)(2,1)S(1)} %get-tuple-element., ...), custom_call_target="tpu_custom_call" | custom-call | tf_op jit(solution)/shard_map/prepare/pallas_call | solution.py:754
  17.6 0.0 collective-permute-done.2.xk.ck
  17.6 0.0 collective-permute-done.1.xc.ccl
  17.7 0.0 collective-permute-done.xr.cr
  17.7 2.5 %fine_forward_kernel.1 = (bf16[1024,128]{1,0:T(8,128)(2,1)S(1)}, bf16[1024,384]{1,0:T(8,128)(2,1)S(1)}, bf16[1024,128]{1,0:T(8,128)(2,1)S(1)}, bf16[16,64,128]{2,1,0:T(8,128)(2,1)S(1)}) custom-call(bf16[16,64,128]{2,1,0:T(8,128)(2,1)S(1)} %get-tuple-element.66.x, bf16[1552,128]{1,0:T(8,128)(2,1)S(1)} %collective-permute-done.xr.cr, ...), custom_call_target="tpu_custom_call" | custom-call | tf_op jit(solution)/shard_map/fine_forward_kernel/pallas_call | solution.py:686
  20.1 3.4 %coarse_kernel.1 = (bf16[2,8,32,128]{3,2,1,0:T(8,128)(2,1)S(1)}, bf16[16,64,128]{2,1,0:T(8,128)(2,1)S(1)}, bf16[256,128]{1,0:T(8,128)(2,1)S(1)}, bf16[64,128]{1,...) custom-call(bf16[16,64,128]{2,1,0:T(8,128)(2,1)S(1)} %get-tuple-elem, ...), custom_call_target="tpu_custom_call" | custom-call | tf_op jit(solution)/shard_map/coarse_kernel/pallas_call | solution.py:686
  23.6 0.1 collective-permute-start.3
  23.7 0.5 collective-permute-start.4
  24.1 0.0 collective-permute-start.5
  24.2 6.0 %collective-permute-done.5.ek = bf16[16,128]{1,0:T(8,128)(2,1)S(1)} collective-permute-done((bf16[16,128]{1,0:T(8,128)(2,1)S(1)}, bf16[16,128]{1,0:T(8,128)(2,1)S(1)}, u32[]{:S(2)}, u32[]{:S(2)}) %collective-permute-start.5) | collective-permute-done | bytes 4128 | tf_op jit(solution)/shard_map/ppermute | solution.py:711
  30.1 0.0 collective-permute-done.4.ec
  30.1 0.0 collective-permute-done.3.er
  30.2 3.6 %fine_backward_kernel.1 = (bf16[16,64,128]{2,1,0:T(8,128)(2,1)S(1)}, bf16[512,128]{1,0:T(8,128)(2,1)S(1)}, bf16[128,128]{1,0:T(8,128)(2,1)S(1)}, bf16[48,128]{1,...) custom-call(bf16[16,64,128]{2,1,0:T(8,128)(2,1)S(1)} %get-tuple-element.85.c, ...), custom_call_target="tpu_custom_call" | custom-call | tf_op jit(solution)/shard_map/fine_backward_kernel/pallas_call | solution.py:686
  33.7 4.4 %collective-permute-start.6 = (f32[2048,128]{1,0:T(8,128)S(1)}, f32[2048,128]{1,0:T(8,128)S(1)}, u32[]{:S(2)}, u32[]{:S(2)}) collective-permute-start(f32[2048,128]{1,0:T(8,128)S(1)} %get-tuple-element.100), channel_id=1, source_target_pairs={{0,1},{1,0},{2,3},{3,2},{4,5},{5,4},{6,7},{7,6},{8,9},{9,8},{10,11... | collective-permute-start | bytes 3145736 | tf_op jit(solution)/shard_map/ppermute | solution.py:802
  38.1 2.3 %collective-permute-done.6.got = f32[2048,128]{1,0:T(8,128)S(1)} collective-permute-done((f32[2048,128]{1,0:T(8,128)S(1)}, f32[2048,128]{1,0:T(8,128)S(1)}, u32[]{:S(2)}, u32[]{:S(2)}) %collective-permute-start.6) | collective-permute-done | bytes 1048608 | tf_op jit(solution)/shard_map/ppermute | solution.py:802
  40.4 1.0 cores_kernel.1
  41.4 9.3 %all-to-all-start = ((bf16[128,16,128]{2,1,0:T(8,128)(2,1)}), bf16[128,16,128]{2,1,0:T(8,128)(2,1)S(1)}, u32[]{:S(2)}, u32[]{:S(2)}) async-start(bf16[128,16,128]{2,1,0:T(8,128)(2,1)} %cores_kernel.1), calls=%async_computation | async-start | bytes 1048576 | tf_op jit(solution)/shard_map/all_to_all | solution.py:716
  50.7 1.4 %collective-permute-start.7 = (bf16[512,128]{1,0:T(8,128)(2,1)S(1)}, bf16[512,128]{1,0:T(8,128)(2,1)S(1)}, u32[]{:S(2)}, u32[]{:S(2)}) collective-permute-start(bf16[512,128]{1,0:T(8,128)(2,1)S(1)} %get-tuple-element.101), channel_id=1, source_target_pairs={{0,1},{1,2},{2,3},{3,4},{4,5},{5,6},{6,7},{7,8},{8,9},{9,10},{10,1... | collective-permute-start | bytes 393224 | tf_op jit(solution)/shard_map/ppermute | solution.py:709
  52.0 1.2 %collective-permute-start.8 = (bf16[128,128]{1,0:T(8,128)(2,1)S(1)}, bf16[128,128]{1,0:T(8,128)(2,1)S(1)}, u32[]{:S(2)}, u32[]{:S(2)}) collective-permute-start(bf16[128,128]{1,0:T(8,128)(2,1)S(1)} %get-tuple-element.102), channel_id=1, source_target_pairs={{0,16},{16,32},{32,48},{48,64},{64,80},{80,96},{96,112},{112,128},... | collective-permute-start | bytes 98312 | tf_op jit(solution)/shard_map/ppermute | solution.py:710
  53.2 1.3 %collective-permute-start.9 = (bf16[48,128]{1,0:T(8,128)(2,1)S(1)}, bf16[48,128]{1,0:T(8,128)(2,1)S(1)}, u32[]{:S(2)}, u32[]{:S(2)}) collective-permute-start(bf16[48,128]{1,0:T(8,128)(2,1)S(1)} %get-tuple-element.103), channel_id=1, source_target_pairs={{0,17},{16,33},{32,49},{48,65},{64,81},{80,97},{96,113},{112,129},... | collective-permute-start | bytes 36872 | tf_op jit(solution)/shard_map/ppermute | solution.py:711
  54.5 13.8 %all-to-all-done.parts = bf16[128,16,128]{2,1,0:T(8,128)(2,1)S(1)} async-done(((bf16[128,16,128]{2,1,0:T(8,128)(2,1)}), bf16[128,16,128]{2,1,0:T(8,128)(2,1)S(1)}, u32[]{:S(2)}, u32[]{:S(2)}) %all-to-all-start) | async-done | bytes 524320 | tf_op jit(solution)/shard_map/all_to_all | solution.py:716
  68.3 0.2 sum_kernel.1
  68.5 0.0 collective-permute-done.9.ek
  68.5 0.0 collective-permute-done.8.ec
  68.5 0.0 collective-permute-done.7.er
  68.5 25.7 %all_to_all.10.own = bf16[128,16,128]{2,1,0:T(8,128)(2,1)S(1)} all-to-all(bf16[128,16,128]{2,1,0:T(8,128)(2,1)S(1)} %sum_kernel.1), channel_id=1, replica_groups=mesh['z'=8,'yl'=2,'yh'=2,'x'=4,'c'=2] {'z','yl','yh','x'}, dimensions={0} | all-to-all | bytes 1048576 | tf_op jit(solution)/shard_map/all_to_all | solution.py:716
  94.2 3.1 %collective-permute-start.10 = (bf16[128,16,128]{2,1,0:T(8,128)(2,1)S(1)}, bf16[128,16,128]{2,1,0:T(8,128)(2,1)S(1)}, u32[]{:S(2)}, u32[]{:S(2)}) collective-permute-start(bf16[128,16,128]{2,1,0:T(8,128)(2,1)S(1)} %all_to_all.10.own), channel_id=1, source_target_pairs={{0,1},{1,0},{2,3},{3,2},{4,5},{5,4},{6,7},{7,6},{8,9},{9,8},{10,11... | collective-permute-start | bytes 1572872 | tf_op jit(solution)/shard_map/ppermute | solution.py:824
  97.3 0.8 place_kernel.1
  98.1 0.7 collective-permute-done.10.got
  98.8 1.3 %unpack_kernel.1 = (f32[1,128]{1,0:T(1,128)}, f32[128,384]{1,0:T(8,128)}, f32[128,128]{1,0:T(8,128)}, f32[4,225]{1,0:T(4,128)}, f32[1,512]{1,0:T(1,128)}, /*inde...) custom-call(bf16[128,16,128]{2,1,0:T(8,128)(2,1)S(1)} %all_to_all.10.own, ...), custom_call_target="tpu_custom_call" | custom-call | tf_op jit(solution)/shard_map/unpack_kernel/pallas_call | solution.py:686
Async XLA Ops:
  1.8 15.8 %collective-permute-start = (bf16[1552,128]{1,0:T(8,128)(2,1)S(1)}, bf16[1552,128]{1,0:T(8,128)(2,1)S(1)}, u32[]{:S(2)}, u32[]{:S(2)}) collective-permute-start(bf16[1552,128]{1,0:T(8,128)(2,1)S(1)} %get-tuple-element.67), channel_id=1, source_target_pairs={{0,15},{1,0},{2,1},{3,2},{4,3},{5,4},{6,5},{7,6},{8,7},{9,8},{10,9... | collective-permute-start | bytes 1191944 | tf_op jit(solution)/shard_map/ppermute | solution.py:709
  5.1 12.5 %collective-permute-start.1 = (bf16[464,128]{1,0:T(8,128)(2,1)S(1)}, bf16[464,128]{1,0:T(8,128)(2,1)S(1)}, u32[]{:S(2)}, u32[]{:S(2)}) collective-permute-start(bf16[464,128]{1,0:T(8,128)(2,1)S(1)} %get-tuple-element.68), channel_id=1, source_target_pairs={{0,240},{16,0},{32,16},{48,32},{64,48},{80,64},{96,80},{112,96},{1... | collective-permute-start | bytes 356360 | tf_op jit(solution)/shard_map/ppermute | solution.py:710
  10.0 7.6 %collective-permute-start.2 = (bf16[304,128]{1,0:T(8,128)(2,1)S(1)}, bf16[304,128]{1,0:T(8,128)(2,1)S(1)}, u32[]{:S(2)}, u32[]{:S(2)}) collective-permute-start(bf16[304,128]{1,0:T(8,128)(2,1)S(1)} %get-tuple-element.69.refs_0_), channel_id=1, source_target_pairs={{0,255},{16,15},{32,31},{48,47},{64,63},{80,79},{96,95},{112,111},... | collective-permute-start | bytes 233480 | tf_op jit(solution)/shard_map/ppermute | solution.py:711
  23.6 6.6 %collective-permute-start.3 = (bf16[256,128]{1,0:T(8,128)(2,1)S(1)}, bf16[256,128]{1,0:T(8,128)(2,1)S(1)}, u32[]{:S(2)}, u32[]{:S(2)}) collective-permute-start(bf16[256,128]{1,0:T(8,128)(2,1)S(1)} %get-tuple-element.87), channel_id=1, source_target_pairs={{0,1},{1,2},{2,3},{3,4},{4,5},{5,6},{6,7},{7,8},{8,9},{9,10},{10,1... | collective-permute-start | bytes 196616 | tf_op jit(solution)/shard_map/ppermute | solution.py:709
  23.7 6.5 %collective-permute-start.4 = (bf16[64,128]{1,0:T(8,128)(2,1)S(1)}, bf16[64,128]{1,0:T(8,128)(2,1)S(1)}, u32[]{:S(2)}, u32[]{:S(2)}) collective-permute-start(bf16[64,128]{1,0:T(8,128)(2,1)S(1)} %get-tuple-element.88), channel_id=1, source_target_pairs={{0,16},{16,32},{32,48},{48,64},{64,80},{80,96},{96,112},{112,128},... | collective-permute-start | bytes 49160 | tf_op jit(solution)/shard_map/ppermute | solution.py:710
  24.1 6.0 %collective-permute-start.5 = (bf16[16,128]{1,0:T(8,128)(2,1)S(1)}, bf16[16,128]{1,0:T(8,128)(2,1)S(1)}, u32[]{:S(2)}, u32[]{:S(2)}) collective-permute-start(bf16[16,128]{1,0:T(8,128)(2,1)S(1)} %get-tuple-element.89), channel_id=1, source_target_pairs={{0,17},{16,33},{32,49},{48,65},{64,81},{80,97},{96,113},{112,129},... | collective-permute-start | bytes 12296 | tf_op jit(solution)/shard_map/ppermute | solution.py:711
  33.7 6.7 %collective-permute-start.6 = (f32[2048,128]{1,0:T(8,128)S(1)}, f32[2048,128]{1,0:T(8,128)S(1)}, u32[]{:S(2)}, u32[]{:S(2)}) collective-permute-start(f32[2048,128]{1,0:T(8,128)S(1)} %get-tuple-element.100), channel_id=1, source_target_pairs={{0,1},{1,0},{2,3},{3,2},{4,5},{5,4},{6,7},{7,6},{8,9},{9,8},{10,11... | collective-permute-start | bytes 3145736 | tf_op jit(solution)/shard_map/ppermute | solution.py:802
  41.4 26.9 %all-to-all-start = ((bf16[128,16,128]{2,1,0:T(8,128)(2,1)}), bf16[128,16,128]{2,1,0:T(8,128)(2,1)S(1)}, u32[]{:S(2)}, u32[]{:S(2)}) async-start(bf16[128,16,128]{2,1,0:T(8,128)(2,1)} %cores_kernel.1), calls=%async_computation | async-start | bytes 1048576 | tf_op jit(solution)/shard_map/all_to_all | solution.py:716
  50.7 17.8 %collective-permute-start.7 = (bf16[512,128]{1,0:T(8,128)(2,1)S(1)}, bf16[512,128]{1,0:T(8,128)(2,1)S(1)}, u32[]{:S(2)}, u32[]{:S(2)}) collective-permute-start(bf16[512,128]{1,0:T(8,128)(2,1)S(1)} %get-tuple-element.101), channel_id=1, source_target_pairs={{0,1},{1,2},{2,3},{3,4},{4,5},{5,6},{6,7},{7,8},{8,9},{9,10},{10,1... | collective-permute-start | bytes 393224 | tf_op jit(solution)/shard_map/ppermute | solution.py:709
  52.0 16.5 %collective-permute-start.8 = (bf16[128,128]{1,0:T(8,128)(2,1)S(1)}, bf16[128,128]{1,0:T(8,128)(2,1)S(1)}, u32[]{:S(2)}, u32[]{:S(2)}) collective-permute-start(bf16[128,128]{1,0:T(8,128)(2,1)S(1)} %get-tuple-element.102), channel_id=1, source_target_pairs={{0,16},{16,32},{32,48},{48,64},{64,80},{80,96},{96,112},{112,128},... | collective-permute-start | bytes 98312 | tf_op jit(solution)/shard_map/ppermute | solution.py:710
  53.2 15.3 %collective-permute-start.9 = (bf16[48,128]{1,0:T(8,128)(2,1)S(1)}, bf16[48,128]{1,0:T(8,128)(2,1)S(1)}, u32[]{:S(2)}, u32[]{:S(2)}) collective-permute-start(bf16[48,128]{1,0:T(8,128)(2,1)S(1)} %get-tuple-element.103), channel_id=1, source_target_pairs={{0,17},{16,33},{32,49},{48,65},{64,81},{80,97},{96,113},{112,129},... | collective-permute-start | bytes 36872 | tf_op jit(solution)/shard_map/ppermute | solution.py:711
  94.2 4.6 %collective-permute-start.10 = (bf16[128,16,128]{2,1,0:T(8,128)(2,1)S(1)}, bf16[128,16,128]{2,1,0:T(8,128)(2,1)S(1)}, u32[]{:S(2)}, u32[]{:S(2)}) collective-permute-start(bf16[128,16,128]{2,1,0:T(8,128)(2,1)S(1)} %all_to_all.10.own), channel_id=1, source_target_pairs={{0,1},{1,0},{2,3},{3,2},{4,5},{5,4},{6,7},{7,6},{8,9},{9,8},{10,11... | collective-permute-start | bytes 1572872 | tf_op jit(solution)/shard_map/ppermute | solution.py:824
